TPU v7x, 512 devices: a whole 4x4x16 slice. The times are simulated.
512 devices in a mesh: seq: 128 (over x, z, core), head: 4 (over y).
Axes of the slice: x: 4, y: 4, z: 16, core: 2. Of those that a mesh axis runs over, the one named last changes fastest.
Arguments:
- query_states: bfloat16 [65536, 2048], P('seq', 'head'), may hold values from -17 to 17
- key_states: bfloat16 [65536, 2048], P('seq', 'head'), may hold values from -10 to 10
- value_states: bfloat16 [65536, 2048], P('seq', 'head'), may hold values from -10 to 10
- output_weight: bfloat16 [2048, 2048], P('head', 'seq'), may hold values from -0.125 to 0.125
Outputs:
- mixed: bfloat16 [65536, 2048], P('seq', 'head')
All inputs are finite; a program needn't handle non-finite values.
Results may differ from a plain program's by a relative error of at most 0.015.
Values may be sent and summed in bfloat16 or wider, within the bound.
No kernel may reach another device: no remote copies, remote signals or barrier semaphores. Data moves between devices by JAX's collectives and lax.ppermute only.
A program may use at most 64 MiB of HBM per device.

v0:
```python
import functools

import jax
import jax.numpy as jnp
from jax import lax
from jax.experimental import pallas as pl
from jax.experimental.pallas import tpu as pltpu
from jax.sharding import Mesh, PartitionSpec as P

HEAD_DIM = 128
BLOCK = 128
GROUP = 16
ROWS = 512
WIDTH = 512
HEADS_HERE = WIDTH // HEAD_DIM
SCALE2 = HEAD_DIM ** (-0.5) * 1.4426950408889634
MASKED = -1e30
F32 = jnp.float32
BF16 = jnp.bfloat16
VMEM_LIMIT = 16 * 1024 * 1024

NT = (((1,), (1,)), ((), ()))
NN = (((1,), (0,)), ((), ()))


def dot(a, b, dims=NN):
    return lax.dot_general(a, b, dims, preferred_element_type=F32)


def iota2(shape, dim):
    return lax.broadcasted_iota(jnp.int32, shape, dim)


def pair_average():
    row, col = iota2((64, 128), 0), iota2((64, 128), 1)
    return jnp.where((col >> 1) == 4 * (row & 15) + (row >> 4), 0.5, 0.0).astype(BF16)


def row_order():
    row, col = iota2((128, 128), 0), iota2((128, 128), 1)
    return jnp.where(col == 8 * (row & 15) + (row >> 4), 1.0, 0.0).astype(BF16)


def row_order_back():
    row, col = iota2((128, 128), 0), iota2((128, 128), 1)
    return jnp.where(row == 8 * (col & 15) + (col >> 4), 1.0, 0.0).astype(BF16)


def halve(x):
    wide = x.astype(F32)
    parts = [
        (wide[32 * i : 32 * i + 16] + wide[32 * i + 16 : 32 * i + 32]) * 0.5
        for i in range(x.shape[0] // 32)
    ]
    out = parts[0] if len(parts) == 1 else jnp.concatenate(parts, axis=0)
    return out.astype(BF16)


def double(x):
    parts = []
    for i in range(x.shape[0] // GROUP):
        piece = x[GROUP * i : GROUP * (i + 1)]
        parts += [piece, piece]
    return jnp.concatenate(parts, axis=0)


def start_copies(sems, pairs):
    copies = [
        pltpu.make_async_copy(source, target, sems.at[i]) for i, (source, target) in enumerate(pairs)
    ]
    for copy in copies:
        copy.start()
    return copies


def coarsen_kernel(
    k_hbm, v_hbm, near_ref, side_ref, own3_ref, kv_ref, sems
):
    core = lax.axis_index("core")
    copies = start_copies(sems, ((k_hbm, kv_ref.at[0]), (v_hbm, kv_ref.at[1])))
    average = pair_average()
    for which, copy in enumerate(copies):
        copy.wait()
        own1 = [dot(average, kv_ref[which, 128 * n : 128 * n + 128, :]).astype(BF16) for n in range(4)]
        own2 = [halve(x) for x in own1]
        own3 = [halve(x) for x in own2]
        for n in range(4):
            own3_ref[which, 16 * n : 16 * n + 16, :] = own3[n]

        def edges(pack_ref, to_left):
            first, second, third, fourth = (0, 1, 2, 3) if to_left else (3, 2, 1, 0)
            pack_ref[which, 0:128, :] = kv_ref[which, 128 * first : 128 * first + 128, :]
            pack_ref[which, 128:192, :] = own1[second]
            pack_ref[which, 192:224, :] = own2[third]
            pack_ref[which, 224:256, :] = own2[fourth]

        def both_edges(near_is_left):
            edges(near_ref, near_is_left)
            edges(side_ref, not near_is_left)

        pl.when(core == 0)(functools.partial(both_edges, True))
        pl.when(core != 0)(functools.partial(both_edges, False))

def unpack(pack_ref, which, average, halo_ref, slot, chips_ref=None):
    edge = pack_ref[which, 0:128, :]
    edge1 = dot(average, edge).astype(BF16)
    next1 = pack_ref[which, 128:192, :]
    rest2 = pack_ref[which, 192:256, :]
    edge2, next2 = halve(edge1), halve(next1)
    pieces = ((0, edge), (128, edge1), (192, next1), (256, edge2), (288, next2), (320, rest2))
    for row, x in pieces:
        halo_ref[which, slot, row : row + x.shape[0], :] = x
    if chips_ref is not None:
        for row, x in ((0, halve(edge2)), (16, halve(next2)), (32, halve(rest2))):
            chips_ref[which, slot, row : row + x.shape[0], :] = x


def prepare_kernel(pack_ref, near_own_ref, own3_ref, near_ref, chip_ref):
    average = pair_average()
    for which in range(2):
        near_ref[which, 0:256, :] = near_own_ref[which]
        chip_ref[which, 0:64, :] = own3_ref[which]
        edge2 = halve(dot(average, pack_ref[which, 0:128, :]).astype(BF16))
        next2 = halve(pack_ref[which, 128:192, :])
        other3 = jnp.concatenate([halve(edge2), halve(next2), halve(pack_ref[which, 192:256, :])], axis=0)
        near_ref[which, 256:320, :] = other3
        chip_ref[which, 64:128, :] = other3


def copies_kernel(piece_ref, gate_hbm, out_ref):
    piece = piece_ref[...]
    for i in range(out_ref.shape[0]):
        out_ref[i] = piece


def gate_kernel(upper_hbm, lower_hbm, upper_out_hbm, lower_out_hbm):
    pass


def stack_kernel(a_hbm, b_hbm, c_hbm, d_hbm, gate_1_hbm, gate_3_hbm, out_hbm, sems):
    sources = (a_hbm, b_hbm, c_hbm, d_hbm)
    for copy in start_copies(sems, [(x, out_hbm.at[i]) for i, x in enumerate(sources)]):
        copy.wait()


def weigh(query, keys, values, bias_left, bias_right):
    scores = dot(query, jnp.concatenate(keys, axis=0), NT)
    if bias_left is not None:
        scores = jnp.concatenate([scores[:, :128] + bias_left, scores[:, 128:]], axis=1)
    if bias_right is not None:
        scores = jnp.concatenate([scores[:, :256], scores[:, 256:] + bias_right], axis=1)
    top = jnp.max(scores, axis=1, keepdims=True)
    probs = jnp.exp2((scores - top) * SCALE2).astype(BF16)
    wide = jnp.concatenate(values, axis=0)
    wide = jnp.concatenate([wide, jnp.ones_like(wide)], axis=1)
    return top, dot(probs, wide)


def merge(fine, coarse):
    fine_top, fine_sums = fine
    top, sums = double(coarse[0]), double(coarse[1])
    fall = jnp.exp2(-jnp.abs(fine_top - top) * SCALE2)
    higher = fine_top >= top
    fine_factor = jnp.where(higher, 1.0, fall)
    factor = jnp.where(higher, fall, 1.0)
    return jnp.maximum(fine_top, top), fine_sums * fine_factor + sums * factor


def attention_kernel(
    q_hbm, k_hbm, v_hbm, side_hbm, chip_hbm, near_hbm, far_hbm, out_ref,
    q_ref, kv_ref, side_ref, chip_ref, near_ref, own1_ref, own2_ref, halo_ref, chips_ref, sems,
):
    core = lax.axis_index("core")
    chip = lax.axis_index(("x", "z"))
    last = lax.axis_size(("x", "z")) - 1
    left_chip = jnp.where(chip > 0, 0.0, MASKED).astype(F32)
    right_chip = jnp.where(chip < last, 0.0, MASKED).astype(F32)
    left_bias = jnp.where(core == 0, left_chip, 0.0)
    right_bias = jnp.where(core == 0, 0.0, right_chip)
    average = pair_average()
    order = row_order()
    back = row_order_back()
    side_slot, near_slot = 1 - core, core
    copies = start_copies(
        sems,
        [
            (k_hbm, kv_ref.at[0]),
            (v_hbm, kv_ref.at[1]),
            (side_hbm, side_ref),
            (near_hbm, near_ref),
            (q_hbm, q_ref),
            (chip_hbm, chip_ref),
        ]
        + [(far_hbm.at[i], chips_ref.at[i, side_slot]) for i in range(2)],
    )
    for which in range(2):
        copies[which].wait()
        for n in range(4):
            own1 = dot(average, kv_ref[which, 128 * n : 128 * n + 128, :]).astype(BF16)
            own1_ref[which, 64 * n : 64 * n + 64, :] = own1
            own2_ref[which, 32 * n : 32 * n + 32, :] = halve(own1)
    copies[2].wait()
    copies[3].wait()
    for which in range(2):
        unpack(side_ref, which, average, halo_ref, side_slot)
        unpack(near_ref, which, average, halo_ref, near_slot, chips_ref)
        chips_ref[which, near_slot, 64:128, :] = near_ref[which, 256:320, :]
    for copy in copies[4:]:
        copy.wait()

    def one_head(head, carry):
        lanes = pl.ds(pl.multiple_of(head * HEAD_DIM, HEAD_DIM), HEAD_DIM)
        q0 = [dot(order, q_ref[128 * n : 128 * n + 128, lanes]).astype(BF16) for n in range(4)]
        q1 = [halve(x) for x in q0]
        q2 = [halve(x) for x in q1]
        q3 = [halve(x) for x in q2]

        def piece(own, which, level, index, count):
            if index < 0:
                return halo_ref[which, 0, 128 * level : 128 * level + 128, lanes]
            if index >= count:
                return halo_ref[which, 1, 128 * level : 128 * level + 128, lanes]
            return own(which, index)

        def own_0(which, index):
            return kv_ref[which, 128 * index : 128 * index + 128, lanes]

        def own_1(which, index):
            return own1_ref[which, 128 * index : 128 * index + 128, lanes]

        def own_2(which, index):
            return own2_ref[which, :, lanes]

        def tile(query, own, level, index, count):
            near = [index - 1, index, index + 1]
            return weigh(
                query,
                [piece(own, 0, level, i, count) for i in near],
                [piece(own, 1, level, i, count) for i in near],
                left_bias if index == 0 else None,
                right_bias if index == count - 1 else None,
            )

        at_3 = weigh(
            jnp.concatenate(q3, axis=0),
            [chips_ref[0, 0, :, lanes], chip_ref[0, :, lanes], chips_ref[0, 1, :, lanes]],
            [chips_ref[1, 0, :, lanes], chip_ref[1, :, lanes], chips_ref[1, 1, :, lanes]],
            left_chip,
            right_chip,
        )
        at_2 = merge(tile(jnp.concatenate(q2, axis=0), own_2, 2, 0, 1), at_3)
        for j in range(2):
            half_2 = tuple(x[64 * j : 64 * j + 64] for x in at_2)
            query_1 = jnp.concatenate(q1[2 * j : 2 * j + 2], axis=0)
            at_1 = merge(tile(query_1, own_1, 1, j, 2), half_2)
            for n in (2 * j, 2 * j + 1):
                start = 64 * (n - 2 * j)
                half_1 = tuple(x[start : start + 64] for x in at_1)
                _, sums = merge(tile(q0[n], own_0, 0, n, 4), half_1)
                attended = (sums[:, :128] / sums[:, 128:]).astype(BF16)
                out_ref[128 * n : 128 * n + 128, lanes] = dot(back, attended).astype(BF16)
        return carry

    lax.fori_loop(0, HEADS_HERE, one_head, 0)


def project_kernel(
    own_hbm, one_hbm, three_hbm, upper_hbm, lower_hbm, mine_hbm, other_hbm,
    out_ref, own_ref, one_ref, three_ref, across_ref, w_ref, sems,
):
    core = lax.axis_index("core")
    twist = lax.axis_index("head") ^ lax.axis_index("x")
    half = ROWS // 2
    order = (0, 1, 3, 2)
    parts = (own_ref, one_ref, three_ref, across_ref)
    stages = [[], [], [], []]
    for stage, i in zip(stages, order):
        for ref, slot in ((mine_hbm, core), (other_hbm, 1 - core)):
            stage.append((ref.at[twist ^ i], w_ref.at[i, :, slot]))
    stages[0].append((own_hbm, own_ref))
    stages[1].append((one_hbm, one_ref))
    stages[2].append((three_hbm, three_ref))
    stages[3].append((upper_hbm, across_ref.at[pl.ds(0, half)]))
    stages[3].append((lower_hbm, across_ref.at[pl.ds(half, half)]))
    copies = start_copies(sems, sum(stages, []))
    for start in (0, half):
        rows = slice(start, start + half)
        total = None
        for at, (ref, i) in enumerate(zip(parts, order)):
            if start == 0:
                for copy in copies[3 * at : 3 * at + len(stages[at])]:
                    copy.wait()
            part = dot(ref[rows, :], w_ref[i].reshape(WIDTH, WIDTH), NT)
            total = part if total is None else total + part
        out_ref[rows, :] = total.astype(BF16)


def call(kernel, outs, args, work_us, scratch=(), copies=(), specs=None, out_spec=pltpu.VMEM, limit=VMEM_LIMIT, aliases=None):
    shapes = [jax.ShapeDtypeStruct(s, BF16) for s in outs]
    one = len(shapes) == 1
    out_specs = [pl.BlockSpec(memory_space=out_spec)] * len(outs)
    return pl.pallas_call(
        kernel,
        out_shape=shapes[0] if one else shapes,
        in_specs=[pl.BlockSpec(memory_space=s) for s in specs or [pl.ANY] * len(args)],
        out_specs=out_specs[0] if one else out_specs,
        scratch_shapes=[pltpu.VMEM(s, BF16) for s in scratch]
        + [pltpu.SemaphoreType.DMA((n,)) for n in copies],
        input_output_aliases=aliases or {},
        cost_estimate=pl.CostEstimate(flops=int(work_us * 1.1e9), bytes_accessed=0, transcendentals=0),
        compiler_params=pltpu.CompilerParams(vmem_limit_bytes=limit),
    )(*args)


def to_all(piece, gate, axis):
    peers = lax.axis_size(axis)
    copies = call(
        copies_kernel,
        [(peers,) + piece.shape],
        (piece, gate),
        1,
        specs=(pltpu.VMEM, pl.ANY),
    )
    return lax.all_to_all(copies, axis, 0, 0, tiled=True)


def on_device(q, k, v, w):
    x_size, z_size = lax.axis_size("x"), lax.axis_size("z")
    count = lax.axis_size("head")
    devices = 2 * x_size * z_size
    seq = ("x", "z", "core")
    swap = [(i, i ^ 1) for i in range(devices)]

    near_own, side_own, own3 = call(
        coarsen_kernel,
        [(2, 256, WIDTH), (2, 256, WIDTH), (2, 64, WIDTH)],
        (k, v),
        3,
        [(2, ROWS, WIDTH)],
        (2,),
    )
    side = lax.ppermute(side_own, seq, swap)
    turn = [(a * count + b, b * count + a) for a in range(x_size) for b in range(count)]
    w_turned = lax.ppermute(w.T, ("x", "head"), turn)

    near, chip3 = call(
        prepare_kernel,
        [(2, 320, WIDTH), (2, 128, WIDTH)],
        (side, near_own, own3),
        2,
        specs=[pltpu.VMEM] * 3,
    )
    to_near = [(i, (i + 1 if i % 2 else i - 1) % devices) for i in range(devices)]
    to_far = [(i, (i - 3 if i % 2 else i + 3) % devices) for i in range(devices)]
    near_in = lax.ppermute(near, seq, to_near)
    far_in = lax.ppermute(chip3, seq, to_far)

    w_z = to_all(w_turned, chip3, "z")

    attended = call(
        attention_kernel,
        [(ROWS, WIDTH)],
        (q, k, v, side, chip3, near_in, far_in),
        11,
        [
            (ROWS, WIDTH), (2, ROWS, WIDTH), (2, 256, WIDTH), (2, 128, WIDTH), (2, 320, WIDTH),
            (2, 256, WIDTH), (2, 128, WIDTH), (2, 2, 384, WIDTH), (2, 2, 128, WIDTH),
        ],
        (8,),
    )
    one = [(i, i ^ 1) for i in range(count)]
    three = [(i, i ^ 3) for i in range(count)]
    half = ROWS // 2
    from_one = lax.ppermute(attended, "head", one)
    from_three = lax.ppermute(attended, "head", three)

    w_x = [w_z] + [
        lax.ppermute(w_z, "x", [(i, i ^ j) for i in range(x_size)]) for j in range(1, x_size)
    ]
    w_mine = call(
        stack_kernel, [(x_size,) + w_z.shape], w_x + [from_one, from_three], 1, (), (x_size,), out_spec=pl.ANY
    )
    w_other = lax.ppermute(w_mine, seq, swap)

    upper = lax.ppermute(from_one[:half], "head", three)
    lower = lax.ppermute(from_three[half:], "head", one)
    upper, lower = call(
        gate_kernel, [upper.shape] * 2, (upper, lower), 8, out_spec=pl.ANY, aliases={0: 0, 1: 1}
    )
    return call(
        project_kernel,
        [(ROWS, WIDTH)],
        (attended, from_one, from_three, upper, lower, w_mine, w_other),
        3,
        [(ROWS, WIDTH)] * 4 + [(count, z_size, 2, 16, WIDTH)],
        (13,),
    )


def solution(mesh):
    count = mesh.shape["head"]
    rows = ("x", "z", "core")
    grid = Mesh(mesh.devices.reshape(4, mesh.shape["seq"] // 8, 2, count), rows + ("head",))
    return jax.shard_map(
        on_device,
        mesh=grid,
        in_specs=(P(rows, "head"), P(rows, "head"), P(rows, "head"), P("head", rows)),
        out_specs=P(rows, "head"),
        check_vma=False,
    )
```

profile of v0, /device:TPU:1, one launch (start us, length us, event | category | flops | bytes accessed | tf_op | source)
XLA Modules:
  0.0 85.7 jit_solution(18278035170599947647)
XLA Ops:
  0.0 0.0 copy-start.1
  0.0 1.0 %copy-done.1 = bf16[512,512]{1,0:T(8,128)(2,1)S(1)} copy-done((bf16[512,512]{1,0:T(8,128)(2,1)S(1)}, bf16[512,512]{1,0:T(8,128)(2,1)}, u32[]{:S(2)}) %copy-start.1) | copy-done | bytes 524312
  1.0 0.0 copy-start.3
  1.0 1.0 %copy-done.3 = bf16[512,512]{1,0:T(8,128)(2,1)S(1)} copy-done((bf16[512,512]{1,0:T(8,128)(2,1)S(1)}, bf16[512,512]{1,0:T(8,128)(2,1)}, u32[]{:S(2)}) %copy-start.3) | copy-done | bytes 524312
  2.1 0.6 shard_map.46
  2.7 8.8 %collective-permute-start = (bf16[2,256,512]{2,1,0:T(8,128)(2,1)S(1)}, bf16[2,256,512]{2,1,0:T(8,128)(2,1)S(1)}, u32[]{:S(2)}, u32[]{:S(2)}) collective-permute-start(bf16[2,256,512]{2,1,0:T(8,128)(2,1)S(1)} %get-tuple-element.12), channel_id=1, source_target_pairs={{0,4},{4,0},{8,12},{12,8},{16,20},{20,16},{24,28},{28,24},{32,36},... | collective-permute-start | bytes 1572872 | tf_op jit(solution)/shard_map/ppermute | solution.py:342
  11.5 1.5 %collective-permute-done.pack_ref.side_hbm = bf16[2,256,512]{2,1,0:T(8,128)(2,1)S(1)} collective-permute-done((bf16[2,256,512]{2,1,0:T(8,128)(2,1)S(1)}, bf16[2,256,512]{2,1,0:T(8,128)(2,1)S(1)}, u32[]{:S(2)}, u32[]{:S(2)}) %collective-permute-start) | collective-permute-done | bytes 524320 | tf_op jit(solution)/shard_map/ppermute | solution.py:342
  13.0 0.0 copy-start.5
  13.0 0.0 copy-start.7
  13.0 0.2 shard_map.47
  13.2 0.6 copy-done.5
  13.8 1.9 %collective-permute-start.1 = (bf16[2,320,512]{2,1,0:T(8,128)(2,1)S(1)}, bf16[2,320,512]{2,1,0:T(8,128)(2,1)S(1)}, u32[]{:S(2)}, u32[]{:S(2)}) collective-permute-start(bf16[2,320,512]{2,1,0:T(8,128)(2,1)S(1)} %get-tuple-element.16), channel_id=1, source_target_pairs={{0,508},{4,8},{8,4},{12,16},{16,12},{20,24},{24,20},{28,32},{32,28... | collective-permute-start | bytes 1966088 | tf_op jit(solution)/shard_map/ppermute | solution.py:355
  15.7 8.9 %collective-permute-start.2 = (bf16[2,128,512]{2,1,0:T(8,128)(2,1)S(1)}, bf16[2,128,512]{2,1,0:T(8,128)(2,1)}, u32[]{:S(2)}, u32[]{:S(2)}) collective-permute-start(bf16[2,128,512]{2,1,0:T(8,128)(2,1)S(1)} %get-tuple-element.15.chip_hbm.gate_hbm), channel_id=1, source_target_pairs={{0,12},{4,504},{8,20},{12,0},{16,28},{20,8},{24,36},{28,16},{32,44... | collective-permute-start | bytes 786440 | tf_op jit(solution)/shard_map/ppermute | solution.py:356
  24.7 0.0 copy-done.7
  24.7 0.7 collective-permute-start.7
  25.4 0.0 collective-permute-done.7.piece_ref
  25.4 0.0 copy-start.2
  25.4 0.0 copy-start.4
  25.4 0.7 shard_map.50
  26.1 0.0 copy-start
  26.1 3.7 %all-to-all-start = ((bf16[16,16,512]{2,1,0:T(8,128)(2,1)}), bf16[16,16,512]{2,1,0:T(8,128)(2,1)S(1)}, u32[]{:S(2)}, u32[]{:S(2)}) async-start(bf16[16,16,512]{2,1,0:T(8,128)(2,1)} %shard_map.50), calls=%async_computation | async-start | bytes 524288 | tf_op jit(solution)/shard_map/all_to_all | solution.py:324
  29.8 2.1 %collective-permute-done.2.far_hbm = bf16[2,128,512]{2,1,0:T(8,128)(2,1)} collective-permute-done((bf16[2,128,512]{2,1,0:T(8,128)(2,1)S(1)}, bf16[2,128,512]{2,1,0:T(8,128)(2,1)}, u32[]{:S(2)}, u32[]{:S(2)}) %collective-permute-start.2) | collective-permute-done | bytes 262176 | tf_op jit(solution)/shard_map/ppermute | solution.py:356
  31.9 0.0 collective-permute-done.1.near_hbm
  31.9 0.0 copy-done.2
  31.9 0.0 copy-done.4
  31.9 0.0 copy-done
  31.9 0.0 copy-start.6
  31.9 1.0 %copy-done.6 = bf16[2,256,512]{2,1,0:T(8,128)(2,1)S(1)} copy-done((bf16[2,256,512]{2,1,0:T(8,128)(2,1)S(1)}, bf16[2,256,512]{2,1,0:T(8,128)(2,1)}, u32[]{:S(2)}) %copy-start.6) | copy-done | bytes 524312
  33.0 11.6 %shard_map.48.own_hbm = bf16[512,512]{1,0:T(8,128)(2,1)} custom-call(bf16[512,512]{1,0:T(8,128)(2,1)S(1)} %copy-done, bf16[512,512]{1,0:T(8,128)(2,1)S(1)} %copy-done.2, bf16[512,512]{1,0:T(8,128)(2,1)S(1)} %copy-done.4, bf16[2,256,512]{2,1,0:T(8,128)(2,1)S(1)} %copy-done.6, bf16[2,128,512]{2,1,0:T(8,128)(2,1)S(1)} %get-tuple-element.15.chip_hbm.gate_hbm, ...), custom_call_target="tpu_custom_call" | custom-call | flops 12099999744 | tf_op jit(solution)/shard_map/pallas_call | solution.py:302
  44.5 10.8 %collective-permute-start.4 = (bf16[512,512]{1,0:T(8,128)(2,1)}, bf16[512,512]{1,0:T(8,128)(2,1)S(1)}, u32[]{:S(2)}, u32[]{:S(2)}) collective-permute-start(bf16[512,512]{1,0:T(8,128)(2,1)} %shard_map.48.own_hbm), channel_id=1, source_target_pairs={{0,3},{1,2},{2,1},{3,0},{4,7},{5,6},{6,5},{7,4},{8,11},{9,10},{10,... | collective-permute-start | bytes 1572872 | tf_op jit(solution)/shard_map/ppermute | solution.py:375
  55.4 1.9 %collective-permute-start.3 = (bf16[512,512]{1,0:T(8,128)(2,1)}, bf16[512,512]{1,0:T(8,128)(2,1)S(1)}, u32[]{:S(2)}, u32[]{:S(2)}) collective-permute-start(bf16[512,512]{1,0:T(8,128)(2,1)} %shard_map.48.own_hbm), channel_id=1, source_target_pairs={{0,1},{1,0},{2,3},{3,2},{4,5},{5,4},{6,7},{7,6},{8,9},{9,8},{10,11... | collective-permute-start | bytes 1572872 | tf_op jit(solution)/shard_map/ppermute | solution.py:374
  57.3 0.0 all-to-all-done.a_hbm
  57.3 5.0 %collective-permute-start.10 = (bf16[16,16,512]{2,1,0:T(8,128)(2,1)S(1)}, bf16[16,16,512]{2,1,0:T(8,128)(2,1)S(1)}, u32[]{:S(2)}, u32[]{:S(2)}) collective-permute-start(bf16[16,16,512]{2,1,0:T(8,128)(2,1)S(1)} %all-to-all-done.a_hbm), channel_id=1, source_target_pairs={{0,384},{128,256},{256,128},{384,0},{1,385},{129,257},{257,129},{3... | collective-permute-start | bytes 786440 | tf_op jit(solution)/shard_map/ppermute | solution.py:378
  62.3 2.7 %collective-permute-start.9 = (bf16[16,16,512]{2,1,0:T(8,128)(2,1)S(1)}, bf16[16,16,512]{2,1,0:T(8,128)(2,1)S(1)}, u32[]{:S(2)}, u32[]{:S(2)}) collective-permute-start(bf16[16,16,512]{2,1,0:T(8,128)(2,1)S(1)} %all-to-all-done.a_hbm), channel_id=1, source_target_pairs={{0,256},{128,384},{256,0},{384,128},{1,257},{129,385},{257,1},{385... | collective-permute-start | bytes 786440 | tf_op jit(solution)/shard_map/ppermute | solution.py:378
  65.1 1.9 %collective-permute-start.8 = (bf16[16,16,512]{2,1,0:T(8,128)(2,1)S(1)}, bf16[16,16,512]{2,1,0:T(8,128)(2,1)S(1)}, u32[]{:S(2)}, u32[]{:S(2)}) collective-permute-start(bf16[16,16,512]{2,1,0:T(8,128)(2,1)S(1)} %all-to-all-done.a_hbm), channel_id=1, source_target_pairs={{0,128},{128,0},{256,384},{384,256},{1,129},{129,1},{257,385},{385... | collective-permute-start | bytes 786440 | tf_op jit(solution)/shard_map/ppermute | solution.py:378
  67.0 0.0 collective-permute-done.4.gate_3_hbm.three_hbm
  67.0 3.4 %collective-permute-start.6 = (bf16[256,512]{1,0:T(8,128)(2,1)S(1)}, bf16[256,512]{1,0:T(8,128)(2,1)S(1)}, u32[]{:S(2)}, u32[]{:S(2)}) collective-permute-start(bf16[256,512]{1,0:T(8,128)(2,1)S(1)} %slice.9), channel_id=1, source_target_pairs={{0,1},{1,0},{2,3},{3,2},{4,5},{5,4},{6,7},{7,6},{8,9},{9,8},{10,11... | collective-permute-start | bytes 786440 | tf_op jit(solution)/shard_map/ppermute | solution.py:386
  70.4 0.0 collective-permute-done.3.gate_1_hbm.one_hbm
  70.5 4.3 %collective-permute-start.5 = (bf16[256,512]{1,0:T(8,128)(2,1)S(1)}, bf16[256,512]{1,0:T(8,128)(2,1)S(1)}, u32[]{:S(2)}, u32[]{:S(2)}) collective-permute-start(bf16[256,512]{1,0:T(8,128)(2,1)S(1)} %slice.8), channel_id=1, source_target_pairs={{0,3},{1,2},{2,1},{3,0},{4,7},{5,6},{6,5},{7,4},{8,11},{9,10},{10,... | collective-permute-start | bytes 786440 | tf_op jit(solution)/shard_map/ppermute | solution.py:385
  74.8 0.0 collective-permute-done.10.d_hbm
  74.8 0.0 collective-permute-done.9.c_hbm
  74.8 0.4 collective-permute-done.8.b_hbm
  75.2 0.1 shard_map.51.mine_hbm
  75.4 4.6 %collective-permute-start.11 = (bf16[4,16,16,512]{3,2,1,0:T(8,128)(2,1)S(1)}, bf16[4,16,16,512]{3,2,1,0:T(8,128)(2,1)S(1)}, u32[]{:S(2)}, u32[]{:S(2)}) collective-permute-start(bf16[4,16,16,512]{3,2,1,0:T(8,128)(2,1)S(1)} %shard_map.51.mine_hbm), channel_id=1, source_target_pairs={{0,4},{4,0},{8,12},{12,8},{16,20},{20,16},{24,28},{28,24},{32,36},... | collective-permute-start | bytes 3145736 | tf_op jit(solution)/shard_map/ppermute | solution.py:383
  80.0 0.0 collective-permute-done.6.lower_hbm
  80.0 0.0 collective-permute-done.5.upper_hbm
  80.0 2.2 %collective-permute-done.11.other_hbm = bf16[4,16,16,512]{3,2,1,0:T(8,128)(2,1)S(1)} collective-permute-done((bf16[4,16,16,512]{3,2,1,0:T(8,128)(2,1)S(1)}, bf16[4,16,16,512]{3,2,1,0:T(8,128)(2,1)S(1)}, u32[]{:S(2)}, u32[]{:S(2)}) %collective-permute-start.11) | collective-permute-done | bytes 1048608 | tf_op jit(solution)/shard_map/ppermute | solution.py:383
  82.3 3.5 %shard_map.52 = bf16[512,512]{1,0:T(8,128)(2,1)} custom-call(bf16[512,512]{1,0:T(8,128)(2,1)} %shard_map.48.own_hbm, bf16[512,512]{1,0:T(8,128)(2,1)S(1)} %collective-permute-done.3.gate_1_hbm.one_hbm, bf16[512,512]{1,0:T(8,128)(2,1)S(1)} %collective-permute-done.4.gate_3_hbm.three_hbm, bf16[256,512]{1,0:T(8,128)(2,1)S(1)} %get-tuple-element.17.upper_hbm, ...), custom_call_target="tpu_custom_call" | custom-call | flops 3300000000 | tf_op jit(solution)/shard_map/pallas_call | solution.py:302
  (3 shorter events, 0.0 us)
Async XLA Ops:
  0.0 1.0 %copy-start.1 = (bf16[512,512]{1,0:T(8,128)(2,1)S(1)}, bf16[512,512]{1,0:T(8,128)(2,1)}, u32[]{:S(2)}) copy-start(bf16[512,512]{1,0:T(8,128)(2,1)} %k_hbm.3) | copy-start | bytes 1572868
  1.0 1.0 %copy-start.3 = (bf16[512,512]{1,0:T(8,128)(2,1)S(1)}, bf16[512,512]{1,0:T(8,128)(2,1)}, u32[]{:S(2)}) copy-start(bf16[512,512]{1,0:T(8,128)(2,1)} %v_hbm.3) | copy-start | bytes 1572868
  2.7 10.3 %collective-permute-start = (bf16[2,256,512]{2,1,0:T(8,128)(2,1)S(1)}, bf16[2,256,512]{2,1,0:T(8,128)(2,1)S(1)}, u32[]{:S(2)}, u32[]{:S(2)}) collective-permute-start(bf16[2,256,512]{2,1,0:T(8,128)(2,1)S(1)} %get-tuple-element.12), channel_id=1, source_target_pairs={{0,4},{4,0},{8,12},{12,8},{16,20},{20,16},{24,28},{28,24},{32,36},... | collective-permute-start | bytes 1572872 | tf_op jit(solution)/shard_map/ppermute | solution.py:342
  13.0 0.8 copy-start.5
  13.0 11.7 %copy-start.7 = (bf16[512,16]{0,1:T(8,128)(2,1)S(1)}, bf16[512,16]{0,1:T(8,128)(2,1)}, u32[]{:S(2)}) copy-start(bf16[512,16]{0,1:T(8,128)(2,1)} %param.7) | copy-start | bytes 49156
  13.8 18.1 %collective-permute-start.1 = (bf16[2,320,512]{2,1,0:T(8,128)(2,1)S(1)}, bf16[2,320,512]{2,1,0:T(8,128)(2,1)S(1)}, u32[]{:S(2)}, u32[]{:S(2)}) collective-permute-start(bf16[2,320,512]{2,1,0:T(8,128)(2,1)S(1)} %get-tuple-element.16), channel_id=1, source_target_pairs={{0,508},{4,8},{8,4},{12,16},{16,12},{20,24},{24,20},{28,32},{32,28... | collective-permute-start | bytes 1966088 | tf_op jit(solution)/shard_map/ppermute | solution.py:355
  15.7 16.2 %collective-permute-start.2 = (bf16[2,128,512]{2,1,0:T(8,128)(2,1)S(1)}, bf16[2,128,512]{2,1,0:T(8,128)(2,1)}, u32[]{:S(2)}, u32[]{:S(2)}) collective-permute-start(bf16[2,128,512]{2,1,0:T(8,128)(2,1)S(1)} %get-tuple-element.15.chip_hbm.gate_hbm), channel_id=1, source_target_pairs={{0,12},{4,504},{8,20},{12,0},{16,28},{20,8},{24,36},{28,16},{32,44... | collective-permute-start | bytes 786440 | tf_op jit(solution)/shard_map/ppermute | solution.py:356
  24.7 0.7 collective-permute-start.7
  25.4 6.5 %copy-start.2 = (bf16[512,512]{1,0:T(8,128)(2,1)S(1)}, bf16[512,512]{1,0:T(8,128)(2,1)}, u32[]{:S(2)}) copy-start(bf16[512,512]{1,0:T(8,128)(2,1)} %k_hbm.3) | copy-start | bytes 1572868
  25.4 6.5 %copy-start.4 = (bf16[512,512]{1,0:T(8,128)(2,1)S(1)}, bf16[512,512]{1,0:T(8,128)(2,1)}, u32[]{:S(2)}) copy-start(bf16[512,512]{1,0:T(8,128)(2,1)} %v_hbm.3) | copy-start | bytes 1572868
  26.1 5.8 %copy-start = (bf16[512,512]{1,0:T(8,128)(2,1)S(1)}, bf16[512,512]{1,0:T(8,128)(2,1)}, u32[]{:S(2)}) copy-start(bf16[512,512]{1,0:T(8,128)(2,1)} %q_hbm.1) | copy-start | bytes 1572868
  26.1 31.1 %all-to-all-start = ((bf16[16,16,512]{2,1,0:T(8,128)(2,1)}), bf16[16,16,512]{2,1,0:T(8,128)(2,1)S(1)}, u32[]{:S(2)}, u32[]{:S(2)}) async-start(bf16[16,16,512]{2,1,0:T(8,128)(2,1)} %shard_map.50), calls=%async_computation | async-start | bytes 524288 | tf_op jit(solution)/shard_map/all_to_all | solution.py:324
  31.9 1.0 %copy-start.6 = (bf16[2,256,512]{2,1,0:T(8,128)(2,1)S(1)}, bf16[2,256,512]{2,1,0:T(8,128)(2,1)}, u32[]{:S(2)}) copy-start(bf16[2,256,512]{2,1,0:T(8,128)(2,1)} %copy-done.5) | copy-start | bytes 1572868
  44.5 22.5 %collective-permute-start.4 = (bf16[512,512]{1,0:T(8,128)(2,1)}, bf16[512,512]{1,0:T(8,128)(2,1)S(1)}, u32[]{:S(2)}, u32[]{:S(2)}) collective-permute-start(bf16[512,512]{1,0:T(8,128)(2,1)} %shard_map.48.own_hbm), channel_id=1, source_target_pairs={{0,3},{1,2},{2,1},{3,0},{4,7},{5,6},{6,5},{7,4},{8,11},{9,10},{10,... | collective-permute-start | bytes 1572872 | tf_op jit(solution)/shard_map/ppermute | solution.py:375
  55.4 15.1 %collective-permute-start.3 = (bf16[512,512]{1,0:T(8,128)(2,1)}, bf16[512,512]{1,0:T(8,128)(2,1)S(1)}, u32[]{:S(2)}, u32[]{:S(2)}) collective-permute-start(bf16[512,512]{1,0:T(8,128)(2,1)} %shard_map.48.own_hbm), channel_id=1, source_target_pairs={{0,1},{1,0},{2,3},{3,2},{4,5},{5,4},{6,7},{7,6},{8,9},{9,8},{10,11... | collective-permute-start | bytes 1572872 | tf_op jit(solution)/shard_map/ppermute | solution.py:374
  57.3 17.5 %collective-permute-start.10 = (bf16[16,16,512]{2,1,0:T(8,128)(2,1)S(1)}, bf16[16,16,512]{2,1,0:T(8,128)(2,1)S(1)}, u32[]{:S(2)}, u32[]{:S(2)}) collective-permute-start(bf16[16,16,512]{2,1,0:T(8,128)(2,1)S(1)} %all-to-all-done.a_hbm), channel_id=1, source_target_pairs={{0,384},{128,256},{256,128},{384,0},{1,385},{129,257},{257,129},{3... | collective-permute-start | bytes 786440 | tf_op jit(solution)/shard_map/ppermute | solution.py:378
  62.3 12.5 %collective-permute-start.9 = (bf16[16,16,512]{2,1,0:T(8,128)(2,1)S(1)}, bf16[16,16,512]{2,1,0:T(8,128)(2,1)S(1)}, u32[]{:S(2)}, u32[]{:S(2)}) collective-permute-start(bf16[16,16,512]{2,1,0:T(8,128)(2,1)S(1)} %all-to-all-done.a_hbm), channel_id=1, source_target_pairs={{0,256},{128,384},{256,0},{384,128},{1,257},{129,385},{257,1},{385... | collective-permute-start | bytes 786440 | tf_op jit(solution)/shard_map/ppermute | solution.py:378
  65.1 10.2 %collective-permute-start.8 = (bf16[16,16,512]{2,1,0:T(8,128)(2,1)S(1)}, bf16[16,16,512]{2,1,0:T(8,128)(2,1)S(1)}, u32[]{:S(2)}, u32[]{:S(2)}) collective-permute-start(bf16[16,16,512]{2,1,0:T(8,128)(2,1)S(1)} %all-to-all-done.a_hbm), channel_id=1, source_target_pairs={{0,128},{128,0},{256,384},{384,256},{1,129},{129,1},{257,385},{385... | collective-permute-start | bytes 786440 | tf_op jit(solution)/shard_map/ppermute | solution.py:378
  67.0 12.9 %collective-permute-start.6 = (bf16[256,512]{1,0:T(8,128)(2,1)S(1)}, bf16[256,512]{1,0:T(8,128)(2,1)S(1)}, u32[]{:S(2)}, u32[]{:S(2)}) collective-permute-start(bf16[256,512]{1,0:T(8,128)(2,1)S(1)} %slice.9), channel_id=1, source_target_pairs={{0,1},{1,0},{2,3},{3,2},{4,5},{5,4},{6,7},{7,6},{8,9},{9,8},{10,11... | collective-permute-start | bytes 786440 | tf_op jit(solution)/shard_map/ppermute | solution.py:386
  70.5 9.5 %collective-permute-start.5 = (bf16[256,512]{1,0:T(8,128)(2,1)S(1)}, bf16[256,512]{1,0:T(8,128)(2,1)S(1)}, u32[]{:S(2)}, u32[]{:S(2)}) collective-permute-start(bf16[256,512]{1,0:T(8,128)(2,1)S(1)} %slice.8), channel_id=1, source_target_pairs={{0,3},{1,2},{2,1},{3,0},{4,7},{5,6},{6,5},{7,4},{8,11},{9,10},{10,... | collective-permute-start | bytes 786440 | tf_op jit(solution)/shard_map/ppermute | solution.py:385
  75.4 6.9 %collective-permute-start.11 = (bf16[4,16,16,512]{3,2,1,0:T(8,128)(2,1)S(1)}, bf16[4,16,16,512]{3,2,1,0:T(8,128)(2,1)S(1)}, u32[]{:S(2)}, u32[]{:S(2)}) collective-permute-start(bf16[4,16,16,512]{3,2,1,0:T(8,128)(2,1)S(1)} %shard_map.51.mine_hbm), channel_id=1, source_target_pairs={{0,4},{4,0},{8,12},{12,8},{16,20},{20,16},{24,28},{28,24},{32,36},... | collective-permute-start | bytes 3145736 | tf_op jit(solution)/shard_map/ppermute | solution.py:383
where the time goes:
time: 86.7 us; the launch traced here: 85.7 us
  starting transfers between devices  58.7 us (68%)
  Pallas kernels  16.7 us (19%)
  waiting for transfers between devices  6.28 us (7%)
  local copies, waits for them, and re-layouts  3.78 us (4%)
    pallas_call x7, Pallas kernels, call(): pl.pallas_call(kernel, out_shape=shapes[0] if one else shapes, in_specs=[...  16.7 us
    ppermute x1, starting transfers between devices, on_device(): from_three = lax.ppermute(attended, 'head', three)  10.8 us
    ppermute x3, starting transfers between devices, on_device(): lax.ppermute(w_z, 'x', [(i, i ^ j) for i in range(x_size)])  9.69 us
    ppermute x1, starting transfers between devices, on_device(): far_in = lax.ppermute(chip3, seq, to_far)  8.94 us
    ppermute x1, starting transfers between devices, on_device(): side = lax.ppermute(side_own, seq, swap)  8.78 us
    ppermute x1, starting transfers between devices, on_device(): w_other = lax.ppermute(w_mine, seq, swap)  4.62 us
    ppermute x1, starting transfers between devices, on_device(): upper = lax.ppermute(from_one[:half], 'head', three)  4.32 us
    unnamed x16, local copies, waits for them, and re-layouts  3.74 us
  transfers between devices with their start and end apart: 13, of which 4 were waited for; matrix products, arithmetic and copies ran while one was open for 0% of the time, Pallas kernels for 15%

commit v1 on v0

--- a/solution.py
+++ b/solution.py
@@ -167,8 +167,8 @@
 
 
 def attention_kernel(
-    q_hbm, k_hbm, v_hbm, side_hbm, chip_hbm, near_hbm, far_hbm, out_ref,
-    q_ref, kv_ref, side_ref, chip_ref, near_ref, own1_ref, own2_ref, halo_ref, chips_ref, sems,
+    q_ref, k_ref, v_ref, side_ref, chip_ref, near_ref, far_ref, out_ref,
+    own1_ref, own2_ref, halo_ref, chips_ref,
 ):
     core = lax.axis_index("core")
     chip = lax.axis_index(("x", "z"))
@@ -181,32 +181,15 @@
     order = row_order()
     back = row_order_back()
     side_slot, near_slot = 1 - core, core
-    copies = start_copies(
-        sems,
-        [
-            (k_hbm, kv_ref.at[0]),
-            (v_hbm, kv_ref.at[1]),
-            (side_hbm, side_ref),
-            (near_hbm, near_ref),
-            (q_hbm, q_ref),
-            (chip_hbm, chip_ref),
-        ]
-        + [(far_hbm.at[i], chips_ref.at[i, side_slot]) for i in range(2)],
-    )
-    for which in range(2):
-        copies[which].wait()
+    for which, ref in enumerate((k_ref, v_ref)):
         for n in range(4):
-            own1 = dot(average, kv_ref[which, 128 * n : 128 * n + 128, :]).astype(BF16)
+            own1 = dot(average, ref[128 * n : 128 * n + 128, :]).astype(BF16)
             own1_ref[which, 64 * n : 64 * n + 64, :] = own1
             own2_ref[which, 32 * n : 32 * n + 32, :] = halve(own1)
-    copies[2].wait()
-    copies[3].wait()
-    for which in range(2):
         unpack(side_ref, which, average, halo_ref, side_slot)
         unpack(near_ref, which, average, halo_ref, near_slot, chips_ref)
         chips_ref[which, near_slot, 64:128, :] = near_ref[which, 256:320, :]
-    for copy in copies[4:]:
-        copy.wait()
+        chips_ref[which, side_slot] = far_ref[which]
 
     def one_head(head, carry):
         lanes = pl.ds(pl.multiple_of(head * HEAD_DIM, HEAD_DIM), HEAD_DIM)
@@ -223,7 +206,7 @@
             return own(which, index)
 
         def own_0(which, index):
-            return kv_ref[which, 128 * index : 128 * index + 128, lanes]
+            return (k_ref, v_ref)[which][128 * index : 128 * index + 128, lanes]
 
         def own_1(which, index):
             return own1_ref[which, 128 * index : 128 * index + 128, lanes]
@@ -261,38 +244,33 @@
                 out_ref[128 * n : 128 * n + 128, lanes] = dot(back, attended).astype(BF16)
         return carry
 
-    lax.fori_loop(0, HEADS_HERE, one_head, 0)
+    lax.fori_loop(0, HEADS_HERE, one_head, 0, unroll=2)
 
 
 def project_kernel(
-    own_hbm, one_hbm, three_hbm, upper_hbm, lower_hbm, mine_hbm, other_hbm,
-    out_ref, own_ref, one_ref, three_ref, across_ref, w_ref, sems,
+    own_ref, one_ref, three_ref, upper_ref, lower_ref, mine_ref, other_ref, out_ref
 ):
     core = lax.axis_index("core")
     twist = lax.axis_index("head") ^ lax.axis_index("x")
     half = ROWS // 2
-    order = (0, 1, 3, 2)
-    parts = (own_ref, one_ref, three_ref, across_ref)
-    stages = [[], [], [], []]
-    for stage, i in zip(stages, order):
-        for ref, slot in ((mine_hbm, core), (other_hbm, 1 - core)):
-            stage.append((ref.at[twist ^ i], w_ref.at[i, :, slot]))
-    stages[0].append((own_hbm, own_ref))
-    stages[1].append((one_hbm, one_ref))
-    stages[2].append((three_hbm, three_ref))
-    stages[3].append((upper_hbm, across_ref.at[pl.ds(0, half)]))
-    stages[3].append((lower_hbm, across_ref.at[pl.ds(half, half)]))
-    copies = start_copies(sems, sum(stages, []))
-    for start in (0, half):
-        rows = slice(start, start + half)
-        total = None
-        for at, (ref, i) in enumerate(zip(parts, order)):
-            if start == 0:
-                for copy in copies[3 * at : 3 * at + len(stages[at])]:
-                    copy.wait()
-            part = dot(ref[rows, :], w_ref[i].reshape(WIDTH, WIDTH), NT)
-            total = part if total is None else total + part
-        out_ref[rows, :] = total.astype(BF16)
+
+    def run(first, second):
+        def weight(i):
+            return jnp.concatenate(
+                [ref[twist ^ i, z] for z in range(first.shape[1]) for ref in (first, second)], axis=0
+            )
+
+        weights = [weight(i) for i in range(4)]
+        for start, across in ((0, upper_ref), (half, lower_ref)):
+            rows = slice(start, start + half)
+            total = dot(own_ref[rows, :], weights[0], NT)
+            total += dot(one_ref[rows, :], weights[1], NT)
+            total += dot(three_ref[rows, :], weights[3], NT)
+            total += dot(across[...], weights[2], NT)
+            out_ref[rows, :] = total.astype(BF16)
+
+    pl.when(core == 0)(functools.partial(run, mine_ref, other_ref))
+    pl.when(core != 0)(functools.partial(run, other_ref, mine_ref))
 
 
 def call(kernel, outs, args, work_us, scratch=(), copies=(), specs=None, out_spec=pltpu.VMEM, limit=VMEM_LIMIT, aliases=None):
@@ -362,12 +340,10 @@
         [(ROWS, WIDTH)],
         (q, k, v, side, chip3, near_in, far_in),
         11,
-        [
-            (ROWS, WIDTH), (2, ROWS, WIDTH), (2, 256, WIDTH), (2, 128, WIDTH), (2, 320, WIDTH),
-            (2, 256, WIDTH), (2, 128, WIDTH), (2, 2, 384, WIDTH), (2, 2, 128, WIDTH),
-        ],
-        (8,),
-    )
+        [(2, 256, WIDTH), (2, 128, WIDTH), (2, 2, 384, WIDTH), (2, 2, 128, WIDTH)],
+        specs=[pltpu.VMEM] * 7,
+    )
+
     one = [(i, i ^ 1) for i in range(count)]
     three = [(i, i ^ 3) for i in range(count)]
     half = ROWS // 2
@@ -392,8 +368,7 @@
         [(ROWS, WIDTH)],
         (attended, from_one, from_three, upper, lower, w_mine, w_other),
         3,
-        [(ROWS, WIDTH)] * 4 + [(count, z_size, 2, 16, WIDTH)],
-        (13,),
+        specs=[pltpu.VMEM] * 7,
     )
 
 

time: 86.7 us -> 86.4 us (level)
  transfers between devices with their start and end apart: 13 -> 13, of which waited for: 4 -> 4; matrix products, arithmetic and copies ran while one was open for 0% -> 0% of each run, Pallas kernels for 15% -> 14%
where the time goes in v1:
time: 86.4 us; the launch traced here: 85.4 us
  starting transfers between devices  58.9 us (68%)
  Pallas kernels  16.1 us (19%)
  waiting for transfers between devices  6.34 us (7%)
  local copies, waits for them, and re-layouts  3.78 us (4%)
    pallas_call x7, Pallas kernels, call(): pl.pallas_call(kernel, out_shape=shapes[0] if one else shapes, in_specs=[...  16.1 us
    ppermute x1, starting transfers between devices, on_device(): from_three = lax.ppermute(attended, 'head', three)  10.8 us
    ppermute x3, starting transfers between devices, on_device(): lax.ppermute(w_z, 'x', [(i, i ^ j) for i in range(x_size)])  9.69 us
    ppermute x1, starting transfers between devices, on_device(): far_in = lax.ppermute(chip3, seq, to_far)  8.94 us
    ppermute x1, starting transfers between devices, on_device(): side = lax.ppermute(side_own, seq, swap)  8.78 us
    ppermute x1, starting transfers between devices, on_device(): w_other = lax.ppermute(w_mine, seq, swap)  4.83 us
    ppermute x1, starting transfers between devices, on_device(): upper = lax.ppermute(from_one[:half], 'head', three)  4.32 us
    unnamed x16, local copies, waits for them, and re-layouts  3.74 us
  transfers between devices with their start and end apart: 13, of which 4 were waited for; matrix products, arithmetic and copies ran while one was open for 0% of the time, Pallas kernels for 14%

profile of v1, /device:TPU:1, one launch (start us, length us, event | category | flops | bytes accessed | tf_op | source)
XLA Modules:
  0.0 85.4 jit_solution(12636996131646498827)
XLA Ops:
  0.0 0.0 copy-start.1
  0.0 1.0 %copy-done.1 = bf16[512,512]{1,0:T(8,128)(2,1)S(1)} copy-done((bf16[512,512]{1,0:T(8,128)(2,1)S(1)}, bf16[512,512]{1,0:T(8,128)(2,1)}, u32[]{:S(2)}) %copy-start.1) | copy-done | bytes 524312
  1.0 0.0 copy-start.3
  1.0 1.0 %copy-done.3 = bf16[512,512]{1,0:T(8,128)(2,1)S(1)} copy-done((bf16[512,512]{1,0:T(8,128)(2,1)S(1)}, bf16[512,512]{1,0:T(8,128)(2,1)}, u32[]{:S(2)}) %copy-start.3) | copy-done | bytes 524312
  2.1 0.6 shard_map.46
  2.7 8.8 %collective-permute-start = (bf16[2,256,512]{2,1,0:T(8,128)(2,1)S(1)}, bf16[2,256,512]{2,1,0:T(8,128)(2,1)S(1)}, u32[]{:S(2)}, u32[]{:S(2)}) collective-permute-start(bf16[2,256,512]{2,1,0:T(8,128)(2,1)S(1)} %get-tuple-element.12), channel_id=1, source_target_pairs={{0,4},{4,0},{8,12},{12,8},{16,20},{20,16},{24,28},{28,24},{32,36},... | collective-permute-start | bytes 1572872 | tf_op jit(solution)/shard_map/ppermute | solution.py:320
  11.5 1.5 %collective-permute-done.pack_ref.side_ref = bf16[2,256,512]{2,1,0:T(8,128)(2,1)S(1)} collective-permute-done((bf16[2,256,512]{2,1,0:T(8,128)(2,1)S(1)}, bf16[2,256,512]{2,1,0:T(8,128)(2,1)S(1)}, u32[]{:S(2)}, u32[]{:S(2)}) %collective-permute-start) | collective-permute-done | bytes 524320 | tf_op jit(solution)/shard_map/ppermute | solution.py:320
  13.0 0.0 copy-start.5
  13.0 0.0 copy-start.7
  13.0 0.2 shard_map.47
  13.2 0.6 copy-done.5
  13.8 1.9 %collective-permute-start.1 = (bf16[2,320,512]{2,1,0:T(8,128)(2,1)S(1)}, bf16[2,320,512]{2,1,0:T(8,128)(2,1)S(1)}, u32[]{:S(2)}, u32[]{:S(2)}) collective-permute-start(bf16[2,320,512]{2,1,0:T(8,128)(2,1)S(1)} %get-tuple-element.16), channel_id=1, source_target_pairs={{0,508},{4,8},{8,4},{12,16},{16,12},{20,24},{24,20},{28,32},{32,28... | collective-permute-start | bytes 1966088 | tf_op jit(solution)/shard_map/ppermute | solution.py:333
  15.7 8.9 %collective-permute-start.2 = (bf16[2,128,512]{2,1,0:T(8,128)(2,1)S(1)}, bf16[2,128,512]{2,1,0:T(8,128)(2,1)}, u32[]{:S(2)}, u32[]{:S(2)}) collective-permute-start(bf16[2,128,512]{2,1,0:T(8,128)(2,1)S(1)} %get-tuple-element.15.chip_ref.gate_hbm), channel_id=1, source_target_pairs={{0,12},{4,504},{8,20},{12,0},{16,28},{20,8},{24,36},{28,16},{32,44... | collective-permute-start | bytes 786440 | tf_op jit(solution)/shard_map/ppermute | solution.py:334
  24.7 0.0 copy-done.7
  24.7 0.7 collective-permute-start.7
  25.4 0.0 collective-permute-done.7.piece_ref
  25.4 0.0 copy-start.2
  25.4 0.0 copy-start.4
  25.4 0.7 shard_map.50
  26.1 0.0 copy-start
  26.1 3.7 %all-to-all-start = ((bf16[16,16,512]{2,1,0:T(8,128)(2,1)}), bf16[16,16,512]{2,1,0:T(8,128)(2,1)S(1)}, u32[]{:S(2)}, u32[]{:S(2)}) async-start(bf16[16,16,512]{2,1,0:T(8,128)(2,1)} %shard_map.50), calls=%async_computation | async-start | bytes 524288 | tf_op jit(solution)/shard_map/all_to_all | solution.py:302
  29.8 2.1 %collective-permute-done.2.far_ref = bf16[2,128,512]{2,1,0:T(8,128)(2,1)} collective-permute-done((bf16[2,128,512]{2,1,0:T(8,128)(2,1)S(1)}, bf16[2,128,512]{2,1,0:T(8,128)(2,1)}, u32[]{:S(2)}, u32[]{:S(2)}) %collective-permute-start.2) | collective-permute-done | bytes 262176 | tf_op jit(solution)/shard_map/ppermute | solution.py:334
  31.9 0.0 collective-permute-done.1.near_ref
  31.9 0.0 copy-done.2
  31.9 0.0 copy-done.4
  31.9 0.0 copy-done
  31.9 0.0 copy-start.6
  31.9 1.0 %copy-done.6 = bf16[2,256,512]{2,1,0:T(8,128)(2,1)S(1)} copy-done((bf16[2,256,512]{2,1,0:T(8,128)(2,1)S(1)}, bf16[2,256,512]{2,1,0:T(8,128)(2,1)}, u32[]{:S(2)}) %copy-start.6) | copy-done | bytes 524312
  33.0 11.3 %shard_map.48.own_ref = bf16[512,512]{1,0:T(8,128)(2,1)} custom-call(bf16[512,512]{1,0:T(8,128)(2,1)S(1)} %copy-done, bf16[512,512]{1,0:T(8,128)(2,1)S(1)} %copy-done.2, bf16[512,512]{1,0:T(8,128)(2,1)S(1)} %copy-done.4, bf16[2,256,512]{2,1,0:T(8,128)(2,1)S(1)} %copy-done.6, bf16[2,128,512]{2,1,0:T(8,128)(2,1)S(1)} %get-tuple-element.15.chip_ref.gate_hbm, ...), custom_call_target="tpu_custom_call" | custom-call | flops 12099999744 | tf_op jit(solution)/shard_map/pallas_call | solution.py:280
  44.3 10.8 %collective-permute-start.4 = (bf16[512,512]{1,0:T(8,128)(2,1)}, bf16[512,512]{1,0:T(8,128)(2,1)S(1)}, u32[]{:S(2)}, u32[]{:S(2)}) collective-permute-start(bf16[512,512]{1,0:T(8,128)(2,1)} %shard_map.48.own_ref), channel_id=1, source_target_pairs={{0,3},{1,2},{2,1},{3,0},{4,7},{5,6},{6,5},{7,4},{8,11},{9,10},{10,... | collective-permute-start | bytes 1572872 | tf_op jit(solution)/shard_map/ppermute | solution.py:351
  55.1 1.9 %collective-permute-start.3 = (bf16[512,512]{1,0:T(8,128)(2,1)}, bf16[512,512]{1,0:T(8,128)(2,1)S(1)}, u32[]{:S(2)}, u32[]{:S(2)}) collective-permute-start(bf16[512,512]{1,0:T(8,128)(2,1)} %shard_map.48.own_ref), channel_id=1, source_target_pairs={{0,1},{1,0},{2,3},{3,2},{4,5},{5,4},{6,7},{7,6},{8,9},{9,8},{10,11... | collective-permute-start | bytes 1572872 | tf_op jit(solution)/shard_map/ppermute | solution.py:350
  57.0 0.0 all-to-all-done.a_hbm
  57.0 5.0 %collective-permute-start.10 = (bf16[16,16,512]{2,1,0:T(8,128)(2,1)S(1)}, bf16[16,16,512]{2,1,0:T(8,128)(2,1)S(1)}, u32[]{:S(2)}, u32[]{:S(2)}) collective-permute-start(bf16[16,16,512]{2,1,0:T(8,128)(2,1)S(1)} %all-to-all-done.a_hbm), channel_id=1, source_target_pairs={{0,384},{128,256},{256,128},{384,0},{1,385},{129,257},{257,129},{3... | collective-permute-start | bytes 786440 | tf_op jit(solution)/shard_map/ppermute | solution.py:354
  62.1 2.7 %collective-permute-start.9 = (bf16[16,16,512]{2,1,0:T(8,128)(2,1)S(1)}, bf16[16,16,512]{2,1,0:T(8,128)(2,1)S(1)}, u32[]{:S(2)}, u32[]{:S(2)}) collective-permute-start(bf16[16,16,512]{2,1,0:T(8,128)(2,1)S(1)} %all-to-all-done.a_hbm), channel_id=1, source_target_pairs={{0,256},{128,384},{256,0},{384,128},{1,257},{129,385},{257,1},{385... | collective-permute-start | bytes 786440 | tf_op jit(solution)/shard_map/ppermute | solution.py:354
  64.8 1.9 %collective-permute-start.8 = (bf16[16,16,512]{2,1,0:T(8,128)(2,1)S(1)}, bf16[16,16,512]{2,1,0:T(8,128)(2,1)S(1)}, u32[]{:S(2)}, u32[]{:S(2)}) collective-permute-start(bf16[16,16,512]{2,1,0:T(8,128)(2,1)S(1)} %all-to-all-done.a_hbm), channel_id=1, source_target_pairs={{0,128},{128,0},{256,384},{384,256},{1,129},{129,1},{257,385},{385... | collective-permute-start | bytes 786440 | tf_op jit(solution)/shard_map/ppermute | solution.py:354
  66.7 0.0 collective-permute-done.4.gate_3_hbm.three_ref
  66.8 3.4 %collective-permute-start.6 = (bf16[256,512]{1,0:T(8,128)(2,1)S(1)}, bf16[256,512]{1,0:T(8,128)(2,1)S(1)}, u32[]{:S(2)}, u32[]{:S(2)}) collective-permute-start(bf16[256,512]{1,0:T(8,128)(2,1)S(1)} %slice.9), channel_id=1, source_target_pairs={{0,1},{1,0},{2,3},{3,2},{4,5},{5,4},{6,7},{7,6},{8,9},{9,8},{10,11... | collective-permute-start | bytes 786440 | tf_op jit(solution)/shard_map/ppermute | solution.py:362
  70.1 0.0 collective-permute-done.3.gate_1_hbm.one_ref
  70.2 4.3 %collective-permute-start.5 = (bf16[256,512]{1,0:T(8,128)(2,1)S(1)}, bf16[256,512]{1,0:T(8,128)(2,1)S(1)}, u32[]{:S(2)}, u32[]{:S(2)}) collective-permute-start(bf16[256,512]{1,0:T(8,128)(2,1)S(1)} %slice.8), channel_id=1, source_target_pairs={{0,3},{1,2},{2,1},{3,0},{4,7},{5,6},{6,5},{7,4},{8,11},{9,10},{10,... | collective-permute-start | bytes 786440 | tf_op jit(solution)/shard_map/ppermute | solution.py:361
  74.5 0.0 collective-permute-done.10.d_hbm
  74.5 0.0 collective-permute-done.9.c_hbm
  74.5 0.5 collective-permute-done.8.b_hbm
  75.0 0.1 shard_map.51.mine_ref
  75.1 4.8 %collective-permute-start.11 = (bf16[4,16,16,512]{3,2,1,0:T(8,128)(2,1)S(1)}, bf16[4,16,16,512]{3,2,1,0:T(8,128)(2,1)S(1)}, u32[]{:S(2)}, u32[]{:S(2)}) collective-permute-start(bf16[4,16,16,512]{3,2,1,0:T(8,128)(2,1)S(1)} %shard_map.51.mine_ref), channel_id=1, source_target_pairs={{0,4},{4,0},{8,12},{12,8},{16,20},{20,16},{24,28},{28,24},{32,36},... | collective-permute-start | bytes 3145736 | tf_op jit(solution)/shard_map/ppermute | solution.py:359
  80.0 0.0 collective-permute-done.6.lower_hbm
  80.0 0.0 collective-permute-done.5.upper_hbm
  80.0 2.2 %collective-permute-done.11.other_ref = bf16[4,16,16,512]{3,2,1,0:T(8,128)(2,1)S(1)} collective-permute-done((bf16[4,16,16,512]{3,2,1,0:T(8,128)(2,1)S(1)}, bf16[4,16,16,512]{3,2,1,0:T(8,128)(2,1)S(1)}, u32[]{:S(2)}, u32[]{:S(2)}) %collective-permute-start.11) | collective-permute-done | bytes 1048608 | tf_op jit(solution)/shard_map/ppermute | solution.py:359
  82.3 3.1 %shard_map.52 = bf16[512,512]{1,0:T(8,128)(2,1)} custom-call(bf16[512,512]{1,0:T(8,128)(2,1)} %shard_map.48.own_ref, bf16[512,512]{1,0:T(8,128)(2,1)S(1)} %collective-permute-done.3.gate_1_hbm.one_ref, bf16[512,512]{1,0:T(8,128)(2,1)S(1)} %collective-permute-done.4.gate_3_hbm.three_ref, bf16[256,512]{1,0:T(8,128)(2,1)S(1)} %get-tuple-element.17.upper_ref, ...), custom_call_target="tpu_custom_call" | custom-call | flops 3300000000 | tf_op jit(solution)/shard_map/pallas_call | solution.py:280
  (3 shorter events, 0.0 us)
Async XLA Ops:
  0.0 1.0 %copy-start.1 = (bf16[512,512]{1,0:T(8,128)(2,1)S(1)}, bf16[512,512]{1,0:T(8,128)(2,1)}, u32[]{:S(2)}) copy-start(bf16[512,512]{1,0:T(8,128)(2,1)} %k_ref.1) | copy-start | bytes 1572868
  1.0 1.0 %copy-start.3 = (bf16[512,512]{1,0:T(8,128)(2,1)S(1)}, bf16[512,512]{1,0:T(8,128)(2,1)}, u32[]{:S(2)}) copy-start(bf16[512,512]{1,0:T(8,128)(2,1)} %v_ref.1) | copy-start | bytes 1572868
  2.7 10.3 %collective-permute-start = (bf16[2,256,512]{2,1,0:T(8,128)(2,1)S(1)}, bf16[2,256,512]{2,1,0:T(8,128)(2,1)S(1)}, u32[]{:S(2)}, u32[]{:S(2)}) collective-permute-start(bf16[2,256,512]{2,1,0:T(8,128)(2,1)S(1)} %get-tuple-element.12), channel_id=1, source_target_pairs={{0,4},{4,0},{8,12},{12,8},{16,20},{20,16},{24,28},{28,24},{32,36},... | collective-permute-start | bytes 1572872 | tf_op jit(solution)/shard_map/ppermute | solution.py:320
  13.0 0.8 copy-start.5
  13.0 11.7 %copy-start.7 = (bf16[512,16]{0,1:T(8,128)(2,1)S(1)}, bf16[512,16]{0,1:T(8,128)(2,1)}, u32[]{:S(2)}) copy-start(bf16[512,16]{0,1:T(8,128)(2,1)} %param.7) | copy-start | bytes 49156
  13.8 18.1 %collective-permute-start.1 = (bf16[2,320,512]{2,1,0:T(8,128)(2,1)S(1)}, bf16[2,320,512]{2,1,0:T(8,128)(2,1)S(1)}, u32[]{:S(2)}, u32[]{:S(2)}) collective-permute-start(bf16[2,320,512]{2,1,0:T(8,128)(2,1)S(1)} %get-tuple-element.16), channel_id=1, source_target_pairs={{0,508},{4,8},{8,4},{12,16},{16,12},{20,24},{24,20},{28,32},{32,28... | collective-permute-start | bytes 1966088 | tf_op jit(solution)/shard_map/ppermute | solution.py:333
  15.7 16.2 %collective-permute-start.2 = (bf16[2,128,512]{2,1,0:T(8,128)(2,1)S(1)}, bf16[2,128,512]{2,1,0:T(8,128)(2,1)}, u32[]{:S(2)}, u32[]{:S(2)}) collective-permute-start(bf16[2,128,512]{2,1,0:T(8,128)(2,1)S(1)} %get-tuple-element.15.chip_ref.gate_hbm), channel_id=1, source_target_pairs={{0,12},{4,504},{8,20},{12,0},{16,28},{20,8},{24,36},{28,16},{32,44... | collective-permute-start | bytes 786440 | tf_op jit(solution)/shard_map/ppermute | solution.py:334
  24.7 0.7 collective-permute-start.7
  25.4 6.5 %copy-start.2 = (bf16[512,512]{1,0:T(8,128)(2,1)S(1)}, bf16[512,512]{1,0:T(8,128)(2,1)}, u32[]{:S(2)}) copy-start(bf16[512,512]{1,0:T(8,128)(2,1)} %k_ref.1) | copy-start | bytes 1572868
  25.4 6.5 %copy-start.4 = (bf16[512,512]{1,0:T(8,128)(2,1)S(1)}, bf16[512,512]{1,0:T(8,128)(2,1)}, u32[]{:S(2)}) copy-start(bf16[512,512]{1,0:T(8,128)(2,1)} %v_ref.1) | copy-start | bytes 1572868
  26.1 5.8 %copy-start = (bf16[512,512]{1,0:T(8,128)(2,1)S(1)}, bf16[512,512]{1,0:T(8,128)(2,1)}, u32[]{:S(2)}) copy-start(bf16[512,512]{1,0:T(8,128)(2,1)} %q_ref.1) | copy-start | bytes 1572868
  26.1 30.9 %all-to-all-start = ((bf16[16,16,512]{2,1,0:T(8,128)(2,1)}), bf16[16,16,512]{2,1,0:T(8,128)(2,1)S(1)}, u32[]{:S(2)}, u32[]{:S(2)}) async-start(bf16[16,16,512]{2,1,0:T(8,128)(2,1)} %shard_map.50), calls=%async_computation | async-start | bytes 524288 | tf_op jit(solution)/shard_map/all_to_all | solution.py:302
  31.9 1.0 %copy-start.6 = (bf16[2,256,512]{2,1,0:T(8,128)(2,1)S(1)}, bf16[2,256,512]{2,1,0:T(8,128)(2,1)}, u32[]{:S(2)}) copy-start(bf16[2,256,512]{2,1,0:T(8,128)(2,1)} %copy-done.5) | copy-start | bytes 1572868
  44.3 22.5 %collective-permute-start.4 = (bf16[512,512]{1,0:T(8,128)(2,1)}, bf16[512,512]{1,0:T(8,128)(2,1)S(1)}, u32[]{:S(2)}, u32[]{:S(2)}) collective-permute-start(bf16[512,512]{1,0:T(8,128)(2,1)} %shard_map.48.own_ref), channel_id=1, source_target_pairs={{0,3},{1,2},{2,1},{3,0},{4,7},{5,6},{6,5},{7,4},{8,11},{9,10},{10,... | collective-permute-start | bytes 1572872 | tf_op jit(solution)/shard_map/ppermute | solution.py:351
  55.1 15.1 %collective-permute-start.3 = (bf16[512,512]{1,0:T(8,128)(2,1)}, bf16[512,512]{1,0:T(8,128)(2,1)S(1)}, u32[]{:S(2)}, u32[]{:S(2)}) collective-permute-start(bf16[512,512]{1,0:T(8,128)(2,1)} %shard_map.48.own_ref), channel_id=1, source_target_pairs={{0,1},{1,0},{2,3},{3,2},{4,5},{5,4},{6,7},{7,6},{8,9},{9,8},{10,11... | collective-permute-start | bytes 1572872 | tf_op jit(solution)/shard_map/ppermute | solution.py:350
  57.0 17.5 %collective-permute-start.10 = (bf16[16,16,512]{2,1,0:T(8,128)(2,1)S(1)}, bf16[16,16,512]{2,1,0:T(8,128)(2,1)S(1)}, u32[]{:S(2)}, u32[]{:S(2)}) collective-permute-start(bf16[16,16,512]{2,1,0:T(8,128)(2,1)S(1)} %all-to-all-done.a_hbm), channel_id=1, source_target_pairs={{0,384},{128,256},{256,128},{384,0},{1,385},{129,257},{257,129},{3... | collective-permute-start | bytes 786440 | tf_op jit(solution)/shard_map/ppermute | solution.py:354
  62.1 12.5 %collective-permute-start.9 = (bf16[16,16,512]{2,1,0:T(8,128)(2,1)S(1)}, bf16[16,16,512]{2,1,0:T(8,128)(2,1)S(1)}, u32[]{:S(2)}, u32[]{:S(2)}) collective-permute-start(bf16[16,16,512]{2,1,0:T(8,128)(2,1)S(1)} %all-to-all-done.a_hbm), channel_id=1, source_target_pairs={{0,256},{128,384},{256,0},{384,128},{1,257},{129,385},{257,1},{385... | collective-permute-start | bytes 786440 | tf_op jit(solution)/shard_map/ppermute | solution.py:354
  64.8 10.2 %collective-permute-start.8 = (bf16[16,16,512]{2,1,0:T(8,128)(2,1)S(1)}, bf16[16,16,512]{2,1,0:T(8,128)(2,1)S(1)}, u32[]{:S(2)}, u32[]{:S(2)}) collective-permute-start(bf16[16,16,512]{2,1,0:T(8,128)(2,1)S(1)} %all-to-all-done.a_hbm), channel_id=1, source_target_pairs={{0,128},{128,0},{256,384},{384,256},{1,129},{129,1},{257,385},{385... | collective-permute-start | bytes 786440 | tf_op jit(solution)/shard_map/ppermute | solution.py:354
  66.8 13.2 %collective-permute-start.6 = (bf16[256,512]{1,0:T(8,128)(2,1)S(1)}, bf16[256,512]{1,0:T(8,128)(2,1)S(1)}, u32[]{:S(2)}, u32[]{:S(2)}) collective-permute-start(bf16[256,512]{1,0:T(8,128)(2,1)S(1)} %slice.9), channel_id=1, source_target_pairs={{0,1},{1,0},{2,3},{3,2},{4,5},{5,4},{6,7},{7,6},{8,9},{9,8},{10,11... | collective-permute-start | bytes 786440 | tf_op jit(solution)/shard_map/ppermute | solution.py:362
  70.2 9.8 %collective-permute-start.5 = (bf16[256,512]{1,0:T(8,128)(2,1)S(1)}, bf16[256,512]{1,0:T(8,128)(2,1)S(1)}, u32[]{:S(2)}, u32[]{:S(2)}) collective-permute-start(bf16[256,512]{1,0:T(8,128)(2,1)S(1)} %slice.8), channel_id=1, source_target_pairs={{0,3},{1,2},{2,1},{3,0},{4,7},{5,6},{6,5},{7,4},{8,11},{9,10},{10,... | collective-permute-start | bytes 786440 | tf_op jit(solution)/shard_map/ppermute | solution.py:361
  75.1 7.1 %collective-permute-start.11 = (bf16[4,16,16,512]{3,2,1,0:T(8,128)(2,1)S(1)}, bf16[4,16,16,512]{3,2,1,0:T(8,128)(2,1)S(1)}, u32[]{:S(2)}, u32[]{:S(2)}) collective-permute-start(bf16[4,16,16,512]{3,2,1,0:T(8,128)(2,1)S(1)} %shard_map.51.mine_ref), channel_id=1, source_target_pairs={{0,4},{4,0},{8,12},{12,8},{16,20},{20,16},{24,28},{28,24},{32,36},... | collective-permute-start | bytes 3145736 | tf_op jit(solution)/shard_map/ppermute | solution.py:359

commit v2 on v1

--- a/solution.py
+++ b/solution.py
@@ -56,12 +56,9 @@
     return out.astype(BF16)
 
 
-def double(x):
-    parts = []
-    for i in range(x.shape[0] // GROUP):
-        piece = x[GROUP * i : GROUP * (i + 1)]
-        parts += [piece, piece]
-    return jnp.concatenate(parts, axis=0)
+def spread(part):
+    row, col = iota2((128, 128), 0), iota2((128, 128), 1)
+    return jnp.where(row == 64 * part + 16 * (col >> 5) + (col & 15), 1.0, 0.0).astype(BF16)
 
 
 def start_copies(sems, pairs):
@@ -144,21 +141,35 @@
 
 
 def weigh(query, keys, values, bias_left, bias_right):
-    scores = dot(query, jnp.concatenate(keys, axis=0), NT)
+    scores = dot(jnp.concatenate(keys, axis=0), query, NT)
     if bias_left is not None:
-        scores = jnp.concatenate([scores[:, :128] + bias_left, scores[:, 128:]], axis=1)
+        scores = jnp.concatenate([scores[:128] + bias_left, scores[128:]], axis=0)
     if bias_right is not None:
-        scores = jnp.concatenate([scores[:, :256], scores[:, 256:] + bias_right], axis=1)
-    top = jnp.max(scores, axis=1, keepdims=True)
+        scores = jnp.concatenate([scores[:256], scores[256:] + bias_right], axis=0)
+    top = jnp.max(scores, axis=0, keepdims=True)
     probs = jnp.exp2((scores - top) * SCALE2).astype(BF16)
-    wide = jnp.concatenate(values, axis=0)
-    wide = jnp.concatenate([wide, jnp.ones_like(wide)], axis=1)
-    return top, dot(probs, wide)
-
-
-def merge(fine, coarse):
+    wide = jnp.concatenate(values, axis=1)
+    wide = jnp.concatenate([wide, jnp.ones((16, wide.shape[1]), BF16)], axis=0)
+    return top, dot(wide, probs)
+
+
+def parts_of(x, count):
+    parts = []
+    for _ in range(count):
+        part = x.astype(BF16)
+        parts.append(part)
+        x = x - part.astype(F32)
+    return parts
+
+
+def merge(fine, coarse, spreading):
     fine_top, fine_sums = fine
-    top, sums = double(coarse[0]), double(coarse[1])
+    rows = fine_sums.shape[0]
+    tops = jnp.broadcast_to(coarse[0], (16,) + coarse[0].shape[1:])
+    doubled = dot(jnp.concatenate(parts_of(coarse[1], 2) + parts_of(tops, 3), axis=0), spreading)
+    sums = doubled[:rows] + doubled[rows : 2 * rows]
+    at = 2 * rows
+    top = doubled[at : at + 1] + doubled[at + 16 : at + 17] + doubled[at + 32 : at + 33]
     fall = jnp.exp2(-jnp.abs(fine_top - top) * SCALE2)
     higher = fine_top >= top
     fine_factor = jnp.where(higher, 1.0, fall)
@@ -180,6 +191,9 @@
     average = pair_average()
     order = row_order()
     back = row_order_back()
+    row, col = iota2((128, 128), 0), iota2((128, 128), 1)
+    same = jnp.where(row == col, 1.0, 0.0).astype(BF16)
+    spreads = [spread(part) for part in range(2)]
     side_slot, near_slot = 1 - core, core
     for which, ref in enumerate((k_ref, v_ref)):
         for n in range(4):
@@ -198,53 +212,51 @@
         q2 = [halve(x) for x in q1]
         q3 = [halve(x) for x in q2]
 
-        def piece(own, which, level, index, count):
+        def own(which, level, index):
+            if level == 0:
+                return (k_ref, v_ref)[which][128 * index : 128 * index + 128, lanes]
+            if level == 1:
+                return own1_ref[which, 128 * index : 128 * index + 128, lanes]
+            return own2_ref[which, :, lanes]
+
+        def piece(which, level, index, count):
+            if level == 3:
+                return chip_ref[which, :, lanes] if index == 0 else chips_ref[which, (index + 1) // 2, :, lanes]
             if index < 0:
                 return halo_ref[which, 0, 128 * level : 128 * level + 128, lanes]
             if index >= count:
                 return halo_ref[which, 1, 128 * level : 128 * level + 128, lanes]
-            return own(which, index)
-
-        def own_0(which, index):
-            return (k_ref, v_ref)[which][128 * index : 128 * index + 128, lanes]
-
-        def own_1(which, index):
-            return own1_ref[which, 128 * index : 128 * index + 128, lanes]
-
-        def own_2(which, index):
-            return own2_ref[which, :, lanes]
-
-        def tile(query, own, level, index, count):
+            return own(which, level, index)
+
+        turned = {}
+
+        def values(level, index, count):
+            if (level, index) not in turned:
+                turned[level, index] = dot(same, piece(1, level, index, count), NT).astype(BF16)
+            return turned[level, index]
+
+        def tile(query, level, index, count, left=left_bias, right=right_bias):
             near = [index - 1, index, index + 1]
             return weigh(
                 query,
-                [piece(own, 0, level, i, count) for i in near],
-                [piece(own, 1, level, i, count) for i in near],
-                left_bias if index == 0 else None,
-                right_bias if index == count - 1 else None,
+                [piece(0, level, i, count) for i in near],
+                [values(level, i, count) for i in near],
+                left if index == 0 else None,
+                right if index == count - 1 else None,
             )
 
-        at_3 = weigh(
-            jnp.concatenate(q3, axis=0),
-            [chips_ref[0, 0, :, lanes], chip_ref[0, :, lanes], chips_ref[0, 1, :, lanes]],
-            [chips_ref[1, 0, :, lanes], chip_ref[1, :, lanes], chips_ref[1, 1, :, lanes]],
-            left_chip,
-            right_chip,
-        )
-        at_2 = merge(tile(jnp.concatenate(q2, axis=0), own_2, 2, 0, 1), at_3)
+        at_3 = tile(jnp.concatenate(q3, axis=0), 3, 0, 1, left_chip, right_chip)
+        at_2 = merge(tile(jnp.concatenate(q2, axis=0), 2, 0, 1), at_3, spreads[0][:64])
         for j in range(2):
-            half_2 = tuple(x[64 * j : 64 * j + 64] for x in at_2)
             query_1 = jnp.concatenate(q1[2 * j : 2 * j + 2], axis=0)
-            at_1 = merge(tile(query_1, own_1, 1, j, 2), half_2)
+            at_1 = merge(tile(query_1, 1, j, 2), at_2, spreads[j])
             for n in (2 * j, 2 * j + 1):
-                start = 64 * (n - 2 * j)
-                half_1 = tuple(x[start : start + 64] for x in at_1)
-                _, sums = merge(tile(q0[n], own_0, 0, n, 4), half_1)
-                attended = (sums[:, :128] / sums[:, 128:]).astype(BF16)
-                out_ref[128 * n : 128 * n + 128, lanes] = dot(back, attended).astype(BF16)
+                _, sums = merge(tile(q0[n], 0, n, 4), at_1, spreads[n - 2 * j])
+                attended = (sums[:128] / sums[128:129]).astype(BF16)
+                out_ref[128 * n : 128 * n + 128, lanes] = dot(back, attended, NT).astype(BF16)
         return carry
 
-    lax.fori_loop(0, HEADS_HERE, one_head, 0, unroll=2)
+    lax.fori_loop(0, HEADS_HERE, one_head, 0)
 
 
 def project_kernel(

time: 86.4 us -> 89.9 us (1.041)
  Pallas kernels: 16.1 us -> 20 us
    pallas_call x7, Pallas kernels: 16.1 us -> 20 us  [call(): pl.pallas_call(kernel, out_shape=shapes[0] if one else shapes, in_specs=[...]
  transfers between devices with their start and end apart: 13 -> 13, of which waited for: 4 -> 4; matrix products, arithmetic and copies ran while one was open for 0% -> 0% of each run, Pallas kernels for 14% -> 18%
where the time goes in v2:
time: 89.9 us; the launch traced here: 88.8 us
  starting transfers between devices  58.4 us (65%)
  Pallas kernels  20 us (22%)
  waiting for transfers between devices  6.36 us (7%)
  local copies, waits for them, and re-layouts  3.78 us (4%)
    pallas_call x7, Pallas kernels, call(): pl.pallas_call(kernel, out_shape=shapes[0] if one else shapes, in_specs=[...  20 us
    ppermute x1, starting transfers between devices, on_device(): from_three = lax.ppermute(attended, 'head', three)  10.8 us
    ppermute x3, starting transfers between devices, on_device(): lax.ppermute(w_z, 'x', [(i, i ^ j) for i in range(x_size)])  9.72 us
    ppermute x1, starting transfers between devices, on_device(): far_in = lax.ppermute(chip3, seq, to_far)  8.94 us
    ppermute x1, starting transfers between devices, on_device(): side = lax.ppermute(side_own, seq, swap)  8.78 us
    ppermute x1, starting transfers between devices, on_device(): w_other = lax.ppermute(w_mine, seq, swap)  4.37 us
    ppermute x1, starting transfers between devices, on_device(): upper = lax.ppermute(from_one[:half], 'head', three)  4.29 us
    unnamed x16, local copies, waits for them, and re-layouts  3.74 us
  transfers between devices with their start and end apart: 13, of which 4 were waited for; matrix products, arithmetic and copies ran while one was open for 0% of the time, Pallas kernels for 18%

profile of v2, /device:TPU:1, one launch (start us, length us, event | category | flops | bytes accessed | tf_op | source)
XLA Modules:
  0.0 88.8 jit_solution(2636156971490056371)
XLA Ops:
  0.0 0.0 copy-start.1
  0.0 1.0 %copy-done.1 = bf16[512,512]{1,0:T(8,128)(2,1)S(1)} copy-done((bf16[512,512]{1,0:T(8,128)(2,1)S(1)}, bf16[512,512]{1,0:T(8,128)(2,1)}, u32[]{:S(2)}) %copy-start.1) | copy-done | bytes 524312
  1.0 0.0 copy-start.3
  1.0 1.0 %copy-done.3 = bf16[512,512]{1,0:T(8,128)(2,1)S(1)} copy-done((bf16[512,512]{1,0:T(8,128)(2,1)S(1)}, bf16[512,512]{1,0:T(8,128)(2,1)}, u32[]{:S(2)}) %copy-start.3) | copy-done | bytes 524312
  2.1 0.6 shard_map.46
  2.7 8.8 %collective-permute-start = (bf16[2,256,512]{2,1,0:T(8,128)(2,1)S(1)}, bf16[2,256,512]{2,1,0:T(8,128)(2,1)S(1)}, u32[]{:S(2)}, u32[]{:S(2)}) collective-permute-start(bf16[2,256,512]{2,1,0:T(8,128)(2,1)S(1)} %get-tuple-element.12), channel_id=1, source_target_pairs={{0,4},{4,0},{8,12},{12,8},{16,20},{20,16},{24,28},{28,24},{32,36},... | collective-permute-start | bytes 1572872 | tf_op jit(solution)/shard_map/ppermute | solution.py:332
  11.5 1.5 %collective-permute-done.pack_ref.side_ref = bf16[2,256,512]{2,1,0:T(8,128)(2,1)S(1)} collective-permute-done((bf16[2,256,512]{2,1,0:T(8,128)(2,1)S(1)}, bf16[2,256,512]{2,1,0:T(8,128)(2,1)S(1)}, u32[]{:S(2)}, u32[]{:S(2)}) %collective-permute-start) | collective-permute-done | bytes 524320 | tf_op jit(solution)/shard_map/ppermute | solution.py:332
  13.0 0.0 copy-start.5
  13.0 0.0 copy-start.7
  13.0 0.2 shard_map.47
  13.2 0.6 copy-done.5
  13.8 1.9 %collective-permute-start.1 = (bf16[2,320,512]{2,1,0:T(8,128)(2,1)S(1)}, bf16[2,320,512]{2,1,0:T(8,128)(2,1)S(1)}, u32[]{:S(2)}, u32[]{:S(2)}) collective-permute-start(bf16[2,320,512]{2,1,0:T(8,128)(2,1)S(1)} %get-tuple-element.16), channel_id=1, source_target_pairs={{0,508},{4,8},{8,4},{12,16},{16,12},{20,24},{24,20},{28,32},{32,28... | collective-permute-start | bytes 1966088 | tf_op jit(solution)/shard_map/ppermute | solution.py:345
  15.7 8.9 %collective-permute-start.2 = (bf16[2,128,512]{2,1,0:T(8,128)(2,1)S(1)}, bf16[2,128,512]{2,1,0:T(8,128)(2,1)}, u32[]{:S(2)}, u32[]{:S(2)}) collective-permute-start(bf16[2,128,512]{2,1,0:T(8,128)(2,1)S(1)} %get-tuple-element.15.chip_ref.gate_hbm), channel_id=1, source_target_pairs={{0,12},{4,504},{8,20},{12,0},{16,28},{20,8},{24,36},{28,16},{32,44... | collective-permute-start | bytes 786440 | tf_op jit(solution)/shard_map/ppermute | solution.py:346
  24.7 0.0 copy-done.7
  24.7 0.7 collective-permute-start.7
  25.4 0.0 collective-permute-done.7.piece_ref
  25.4 0.0 copy-start.2
  25.4 0.0 copy-start.4
  25.4 0.7 shard_map.50
  26.1 0.0 copy-start
  26.1 3.7 %all-to-all-start = ((bf16[16,16,512]{2,1,0:T(8,128)(2,1)}), bf16[16,16,512]{2,1,0:T(8,128)(2,1)S(1)}, u32[]{:S(2)}, u32[]{:S(2)}) async-start(bf16[16,16,512]{2,1,0:T(8,128)(2,1)} %shard_map.50), calls=%async_computation | async-start | bytes 524288 | tf_op jit(solution)/shard_map/all_to_all | solution.py:314
  29.8 2.1 %collective-permute-done.2.far_ref = bf16[2,128,512]{2,1,0:T(8,128)(2,1)} collective-permute-done((bf16[2,128,512]{2,1,0:T(8,128)(2,1)S(1)}, bf16[2,128,512]{2,1,0:T(8,128)(2,1)}, u32[]{:S(2)}, u32[]{:S(2)}) %collective-permute-start.2) | collective-permute-done | bytes 262176 | tf_op jit(solution)/shard_map/ppermute | solution.py:346
  31.9 0.0 collective-permute-done.1.near_ref
  31.9 0.0 copy-done.2
  31.9 0.0 copy-done.4
  31.9 0.0 copy-done
  31.9 0.0 copy-start.6
  31.9 1.0 %copy-done.6 = bf16[2,256,512]{2,1,0:T(8,128)(2,1)S(1)} copy-done((bf16[2,256,512]{2,1,0:T(8,128)(2,1)S(1)}, bf16[2,256,512]{2,1,0:T(8,128)(2,1)}, u32[]{:S(2)}) %copy-start.6) | copy-done | bytes 524312
  33.0 15.2 %shard_map.48.own_ref = bf16[512,512]{1,0:T(8,128)(2,1)} custom-call(bf16[512,512]{1,0:T(8,128)(2,1)S(1)} %copy-done, bf16[512,512]{1,0:T(8,128)(2,1)S(1)} %copy-done.2, bf16[512,512]{1,0:T(8,128)(2,1)S(1)} %copy-done.4, bf16[2,256,512]{2,1,0:T(8,128)(2,1)S(1)} %copy-done.6, bf16[2,128,512]{2,1,0:T(8,128)(2,1)S(1)} %get-tuple-element.15.chip_ref.gate_hbm, ...), custom_call_target="tpu_custom_call" | custom-call | flops 12099999744 | tf_op jit(solution)/shard_map/pallas_call | solution.py:292
  48.2 10.8 %collective-permute-start.4 = (bf16[512,512]{1,0:T(8,128)(2,1)}, bf16[512,512]{1,0:T(8,128)(2,1)S(1)}, u32[]{:S(2)}, u32[]{:S(2)}) collective-permute-start(bf16[512,512]{1,0:T(8,128)(2,1)} %shard_map.48.own_ref), channel_id=1, source_target_pairs={{0,3},{1,2},{2,1},{3,0},{4,7},{5,6},{6,5},{7,4},{8,11},{9,10},{10,... | collective-permute-start | bytes 1572872 | tf_op jit(solution)/shard_map/ppermute | solution.py:363
  59.0 1.9 %collective-permute-start.3 = (bf16[512,512]{1,0:T(8,128)(2,1)}, bf16[512,512]{1,0:T(8,128)(2,1)S(1)}, u32[]{:S(2)}, u32[]{:S(2)}) collective-permute-start(bf16[512,512]{1,0:T(8,128)(2,1)} %shard_map.48.own_ref), channel_id=1, source_target_pairs={{0,1},{1,0},{2,3},{3,2},{4,5},{5,4},{6,7},{7,6},{8,9},{9,8},{10,11... | collective-permute-start | bytes 1572872 | tf_op jit(solution)/shard_map/ppermute | solution.py:362
  60.9 0.0 all-to-all-done.a_hbm
  60.9 5.0 %collective-permute-start.10 = (bf16[16,16,512]{2,1,0:T(8,128)(2,1)S(1)}, bf16[16,16,512]{2,1,0:T(8,128)(2,1)S(1)}, u32[]{:S(2)}, u32[]{:S(2)}) collective-permute-start(bf16[16,16,512]{2,1,0:T(8,128)(2,1)S(1)} %all-to-all-done.a_hbm), channel_id=1, source_target_pairs={{0,384},{128,256},{256,128},{384,0},{1,385},{129,257},{257,129},{3... | collective-permute-start | bytes 786440 | tf_op jit(solution)/shard_map/ppermute | solution.py:366
  66.0 2.8 %collective-permute-start.9 = (bf16[16,16,512]{2,1,0:T(8,128)(2,1)S(1)}, bf16[16,16,512]{2,1,0:T(8,128)(2,1)S(1)}, u32[]{:S(2)}, u32[]{:S(2)}) collective-permute-start(bf16[16,16,512]{2,1,0:T(8,128)(2,1)S(1)} %all-to-all-done.a_hbm), channel_id=1, source_target_pairs={{0,256},{128,384},{256,0},{384,128},{1,257},{129,385},{257,1},{385... | collective-permute-start | bytes 786440 | tf_op jit(solution)/shard_map/ppermute | solution.py:366
  68.7 1.9 %collective-permute-start.8 = (bf16[16,16,512]{2,1,0:T(8,128)(2,1)S(1)}, bf16[16,16,512]{2,1,0:T(8,128)(2,1)S(1)}, u32[]{:S(2)}, u32[]{:S(2)}) collective-permute-start(bf16[16,16,512]{2,1,0:T(8,128)(2,1)S(1)} %all-to-all-done.a_hbm), channel_id=1, source_target_pairs={{0,128},{128,0},{256,384},{384,256},{1,129},{129,1},{257,385},{385... | collective-permute-start | bytes 786440 | tf_op jit(solution)/shard_map/ppermute | solution.py:366
  70.7 0.0 collective-permute-done.4.gate_3_hbm.three_ref
  70.7 3.4 %collective-permute-start.6 = (bf16[256,512]{1,0:T(8,128)(2,1)S(1)}, bf16[256,512]{1,0:T(8,128)(2,1)S(1)}, u32[]{:S(2)}, u32[]{:S(2)}) collective-permute-start(bf16[256,512]{1,0:T(8,128)(2,1)S(1)} %slice.9), channel_id=1, source_target_pairs={{0,1},{1,0},{2,3},{3,2},{4,5},{5,4},{6,7},{7,6},{8,9},{9,8},{10,11... | collective-permute-start | bytes 786440 | tf_op jit(solution)/shard_map/ppermute | solution.py:374
  74.1 0.0 collective-permute-done.3.gate_1_hbm.one_ref
  74.1 4.3 %collective-permute-start.5 = (bf16[256,512]{1,0:T(8,128)(2,1)S(1)}, bf16[256,512]{1,0:T(8,128)(2,1)S(1)}, u32[]{:S(2)}, u32[]{:S(2)}) collective-permute-start(bf16[256,512]{1,0:T(8,128)(2,1)S(1)} %slice.8), channel_id=1, source_target_pairs={{0,3},{1,2},{2,1},{3,0},{4,7},{5,6},{6,5},{7,4},{8,11},{9,10},{10,... | collective-permute-start | bytes 786440 | tf_op jit(solution)/shard_map/ppermute | solution.py:373
  78.4 0.0 collective-permute-done.10.d_hbm
  78.4 0.0 collective-permute-done.9.c_hbm
  78.4 0.5 collective-permute-done.8.b_hbm
  79.0 0.1 shard_map.51.mine_ref
  79.1 4.4 %collective-permute-start.11 = (bf16[4,16,16,512]{3,2,1,0:T(8,128)(2,1)S(1)}, bf16[4,16,16,512]{3,2,1,0:T(8,128)(2,1)S(1)}, u32[]{:S(2)}, u32[]{:S(2)}) collective-permute-start(bf16[4,16,16,512]{3,2,1,0:T(8,128)(2,1)S(1)} %shard_map.51.mine_ref), channel_id=1, source_target_pairs={{0,4},{4,0},{8,12},{12,8},{16,20},{20,16},{24,28},{28,24},{32,36},... | collective-permute-start | bytes 3145736 | tf_op jit(solution)/shard_map/ppermute | solution.py:371
  83.5 0.0 collective-permute-done.6.lower_hbm
  83.5 0.0 collective-permute-done.5.upper_hbm
  83.5 2.2 %collective-permute-done.11.other_ref = bf16[4,16,16,512]{3,2,1,0:T(8,128)(2,1)S(1)} collective-permute-done((bf16[4,16,16,512]{3,2,1,0:T(8,128)(2,1)S(1)}, bf16[4,16,16,512]{3,2,1,0:T(8,128)(2,1)S(1)}, u32[]{:S(2)}, u32[]{:S(2)}) %collective-permute-start.11) | collective-permute-done | bytes 1048608 | tf_op jit(solution)/shard_map/ppermute | solution.py:371
  85.7 3.1 %shard_map.52 = bf16[512,512]{1,0:T(8,128)(2,1)} custom-call(bf16[512,512]{1,0:T(8,128)(2,1)} %shard_map.48.own_ref, bf16[512,512]{1,0:T(8,128)(2,1)S(1)} %collective-permute-done.3.gate_1_hbm.one_ref, bf16[512,512]{1,0:T(8,128)(2,1)S(1)} %collective-permute-done.4.gate_3_hbm.three_ref, bf16[256,512]{1,0:T(8,128)(2,1)S(1)} %get-tuple-element.17.upper_ref, ...), custom_call_target="tpu_custom_call" | custom-call | flops 3300000000 | tf_op jit(solution)/shard_map/pallas_call | solution.py:292
  (3 shorter events, 0.0 us)
Async XLA Ops:
  0.0 1.0 %copy-start.1 = (bf16[512,512]{1,0:T(8,128)(2,1)S(1)}, bf16[512,512]{1,0:T(8,128)(2,1)}, u32[]{:S(2)}) copy-start(bf16[512,512]{1,0:T(8,128)(2,1)} %k_ref.1) | copy-start | bytes 1572868
  1.0 1.0 %copy-start.3 = (bf16[512,512]{1,0:T(8,128)(2,1)S(1)}, bf16[512,512]{1,0:T(8,128)(2,1)}, u32[]{:S(2)}) copy-start(bf16[512,512]{1,0:T(8,128)(2,1)} %v_ref.1) | copy-start | bytes 1572868
  2.7 10.3 %collective-permute-start = (bf16[2,256,512]{2,1,0:T(8,128)(2,1)S(1)}, bf16[2,256,512]{2,1,0:T(8,128)(2,1)S(1)}, u32[]{:S(2)}, u32[]{:S(2)}) collective-permute-start(bf16[2,256,512]{2,1,0:T(8,128)(2,1)S(1)} %get-tuple-element.12), channel_id=1, source_target_pairs={{0,4},{4,0},{8,12},{12,8},{16,20},{20,16},{24,28},{28,24},{32,36},... | collective-permute-start | bytes 1572872 | tf_op jit(solution)/shard_map/ppermute | solution.py:332
  13.0 0.8 copy-start.5
  13.0 11.7 %copy-start.7 = (bf16[512,16]{0,1:T(8,128)(2,1)S(1)}, bf16[512,16]{0,1:T(8,128)(2,1)}, u32[]{:S(2)}) copy-start(bf16[512,16]{0,1:T(8,128)(2,1)} %param.7) | copy-start | bytes 49156
  13.8 18.1 %collective-permute-start.1 = (bf16[2,320,512]{2,1,0:T(8,128)(2,1)S(1)}, bf16[2,320,512]{2,1,0:T(8,128)(2,1)S(1)}, u32[]{:S(2)}, u32[]{:S(2)}) collective-permute-start(bf16[2,320,512]{2,1,0:T(8,128)(2,1)S(1)} %get-tuple-element.16), channel_id=1, source_target_pairs={{0,508},{4,8},{8,4},{12,16},{16,12},{20,24},{24,20},{28,32},{32,28... | collective-permute-start | bytes 1966088 | tf_op jit(solution)/shard_map/ppermute | solution.py:345
  15.7 16.2 %collective-permute-start.2 = (bf16[2,128,512]{2,1,0:T(8,128)(2,1)S(1)}, bf16[2,128,512]{2,1,0:T(8,128)(2,1)}, u32[]{:S(2)}, u32[]{:S(2)}) collective-permute-start(bf16[2,128,512]{2,1,0:T(8,128)(2,1)S(1)} %get-tuple-element.15.chip_ref.gate_hbm), channel_id=1, source_target_pairs={{0,12},{4,504},{8,20},{12,0},{16,28},{20,8},{24,36},{28,16},{32,44... | collective-permute-start | bytes 786440 | tf_op jit(solution)/shard_map/ppermute | solution.py:346
  24.7 0.7 collective-permute-start.7
  25.4 6.5 %copy-start.2 = (bf16[512,512]{1,0:T(8,128)(2,1)S(1)}, bf16[512,512]{1,0:T(8,128)(2,1)}, u32[]{:S(2)}) copy-start(bf16[512,512]{1,0:T(8,128)(2,1)} %k_ref.1) | copy-start | bytes 1572868
  25.4 6.5 %copy-start.4 = (bf16[512,512]{1,0:T(8,128)(2,1)S(1)}, bf16[512,512]{1,0:T(8,128)(2,1)}, u32[]{:S(2)}) copy-start(bf16[512,512]{1,0:T(8,128)(2,1)} %v_ref.1) | copy-start | bytes 1572868
  26.1 5.8 %copy-start = (bf16[512,512]{1,0:T(8,128)(2,1)S(1)}, bf16[512,512]{1,0:T(8,128)(2,1)}, u32[]{:S(2)}) copy-start(bf16[512,512]{1,0:T(8,128)(2,1)} %q_ref.1) | copy-start | bytes 1572868
  26.1 34.8 %all-to-all-start = ((bf16[16,16,512]{2,1,0:T(8,128)(2,1)}), bf16[16,16,512]{2,1,0:T(8,128)(2,1)S(1)}, u32[]{:S(2)}, u32[]{:S(2)}) async-start(bf16[16,16,512]{2,1,0:T(8,128)(2,1)} %shard_map.50), calls=%async_computation | async-start | bytes 524288 | tf_op jit(solution)/shard_map/all_to_all | solution.py:314
  31.9 1.0 %copy-start.6 = (bf16[2,256,512]{2,1,0:T(8,128)(2,1)S(1)}, bf16[2,256,512]{2,1,0:T(8,128)(2,1)}, u32[]{:S(2)}) copy-start(bf16[2,256,512]{2,1,0:T(8,128)(2,1)} %copy-done.5) | copy-start | bytes 1572868
  48.2 22.5 %collective-permute-start.4 = (bf16[512,512]{1,0:T(8,128)(2,1)}, bf16[512,512]{1,0:T(8,128)(2,1)S(1)}, u32[]{:S(2)}, u32[]{:S(2)}) collective-permute-start(bf16[512,512]{1,0:T(8,128)(2,1)} %shard_map.48.own_ref), channel_id=1, source_target_pairs={{0,3},{1,2},{2,1},{3,0},{4,7},{5,6},{6,5},{7,4},{8,11},{9,10},{10,... | collective-permute-start | bytes 1572872 | tf_op jit(solution)/shard_map/ppermute | solution.py:363
  59.0 15.1 %collective-permute-start.3 = (bf16[512,512]{1,0:T(8,128)(2,1)}, bf16[512,512]{1,0:T(8,128)(2,1)S(1)}, u32[]{:S(2)}, u32[]{:S(2)}) collective-permute-start(bf16[512,512]{1,0:T(8,128)(2,1)} %shard_map.48.own_ref), channel_id=1, source_target_pairs={{0,1},{1,0},{2,3},{3,2},{4,5},{5,4},{6,7},{7,6},{8,9},{9,8},{10,11... | collective-permute-start | bytes 1572872 | tf_op jit(solution)/shard_map/ppermute | solution.py:362
  60.9 17.5 %collective-permute-start.10 = (bf16[16,16,512]{2,1,0:T(8,128)(2,1)S(1)}, bf16[16,16,512]{2,1,0:T(8,128)(2,1)S(1)}, u32[]{:S(2)}, u32[]{:S(2)}) collective-permute-start(bf16[16,16,512]{2,1,0:T(8,128)(2,1)S(1)} %all-to-all-done.a_hbm), channel_id=1, source_target_pairs={{0,384},{128,256},{256,128},{384,0},{1,385},{129,257},{257,129},{3... | collective-permute-start | bytes 786440 | tf_op jit(solution)/shard_map/ppermute | solution.py:366
  66.0 12.5 %collective-permute-start.9 = (bf16[16,16,512]{2,1,0:T(8,128)(2,1)S(1)}, bf16[16,16,512]{2,1,0:T(8,128)(2,1)S(1)}, u32[]{:S(2)}, u32[]{:S(2)}) collective-permute-start(bf16[16,16,512]{2,1,0:T(8,128)(2,1)S(1)} %all-to-all-done.a_hbm), channel_id=1, source_target_pairs={{0,256},{128,384},{256,0},{384,128},{1,257},{129,385},{257,1},{385... | collective-permute-start | bytes 786440 | tf_op jit(solution)/shard_map/ppermute | solution.py:366
  68.7 10.2 %collective-permute-start.8 = (bf16[16,16,512]{2,1,0:T(8,128)(2,1)S(1)}, bf16[16,16,512]{2,1,0:T(8,128)(2,1)S(1)}, u32[]{:S(2)}, u32[]{:S(2)}) collective-permute-start(bf16[16,16,512]{2,1,0:T(8,128)(2,1)S(1)} %all-to-all-done.a_hbm), channel_id=1, source_target_pairs={{0,128},{128,0},{256,384},{384,256},{1,129},{129,1},{257,385},{385... | collective-permute-start | bytes 786440 | tf_op jit(solution)/shard_map/ppermute | solution.py:366
  70.7 12.7 %collective-permute-start.6 = (bf16[256,512]{1,0:T(8,128)(2,1)S(1)}, bf16[256,512]{1,0:T(8,128)(2,1)S(1)}, u32[]{:S(2)}, u32[]{:S(2)}) collective-permute-start(bf16[256,512]{1,0:T(8,128)(2,1)S(1)} %slice.9), channel_id=1, source_target_pairs={{0,1},{1,0},{2,3},{3,2},{4,5},{5,4},{6,7},{7,6},{8,9},{9,8},{10,11... | collective-permute-start | bytes 786440 | tf_op jit(solution)/shard_map/ppermute | solution.py:374
  74.1 9.3 %collective-permute-start.5 = (bf16[256,512]{1,0:T(8,128)(2,1)S(1)}, bf16[256,512]{1,0:T(8,128)(2,1)S(1)}, u32[]{:S(2)}, u32[]{:S(2)}) collective-permute-start(bf16[256,512]{1,0:T(8,128)(2,1)S(1)} %slice.8), channel_id=1, source_target_pairs={{0,3},{1,2},{2,1},{3,0},{4,7},{5,6},{6,5},{7,4},{8,11},{9,10},{10,... | collective-permute-start | bytes 786440 | tf_op jit(solution)/shard_map/ppermute | solution.py:373
  79.1 6.6 %collective-permute-start.11 = (bf16[4,16,16,512]{3,2,1,0:T(8,128)(2,1)S(1)}, bf16[4,16,16,512]{3,2,1,0:T(8,128)(2,1)S(1)}, u32[]{:S(2)}, u32[]{:S(2)}) collective-permute-start(bf16[4,16,16,512]{3,2,1,0:T(8,128)(2,1)S(1)} %shard_map.51.mine_ref), channel_id=1, source_target_pairs={{0,4},{4,0},{8,12},{12,8},{16,20},{20,16},{24,28},{28,24},{32,36},... | collective-permute-start | bytes 3145736 | tf_op jit(solution)/shard_map/ppermute | solution.py:371

commit v3 on v1

--- a/solution.py
+++ b/solution.py
@@ -134,6 +134,10 @@
 
 
 def gate_kernel(upper_hbm, lower_hbm, upper_out_hbm, lower_out_hbm):
+    pass
+
+
+def hold_kernel(value_hbm, out_hbm):
     pass
 
 
@@ -320,6 +324,7 @@
     side = lax.ppermute(side_own, seq, swap)
     turn = [(a * count + b, b * count + a) for a in range(x_size) for b in range(count)]
     w_turned = lax.ppermute(w.T, ("x", "head"), turn)
+    w_turned = call(hold_kernel, [w_turned.shape], (w_turned,), 3, out_spec=pl.ANY, aliases={0: 0})
 
     near, chip3 = call(
         prepare_kernel,
@@ -328,10 +333,10 @@
         2,
         specs=[pltpu.VMEM] * 3,
     )
-    to_near = [(i, (i + 1 if i % 2 else i - 1) % devices) for i in range(devices)]
-    to_far = [(i, (i - 3 if i % 2 else i + 3) % devices) for i in range(devices)]
+    to_near = [(i, i + 1 if i % 2 else i - 1) for i in range(1, devices - 1)]
+    to_far = [(i, j) for i in range(devices) for j in [i - 3 if i % 2 else i + 3] if 0 <= j < devices]
+    far_in = lax.ppermute(chip3, seq, to_far)
     near_in = lax.ppermute(near, seq, to_near)
-    far_in = lax.ppermute(chip3, seq, to_far)
 
     w_z = to_all(w_turned, chip3, "z")
 

time: 86.4 us -> 85.3 us (0.987)
  starting transfers between devices: 58.9 us -> 57.7 us
    all_to_all x1, starting transfers between devices: 3.66 us -> 11.3 us  [to_all(): return lax.all_to_all(copies, axis, 0, 0, tiled=True)]
    ppermute x1, starting transfers between devices: 8.94 us -> 1.37 us  [on_device(): far_in = lax.ppermute(chip3, seq, to_far)]
    ppermute x1, starting transfers between devices: 4.32 us -> 1.92 us  [on_device(): upper = lax.ppermute(from_one[:half], 'head', three)]
    ppermute x3, waiting for transfers between devices: 0.5 us -> 2.7 us  [on_device(): lax.ppermute(w_z, 'x', [(i, i ^ j) for i in range(x_size)])]
    ppermute x3, starting transfers between devices: 9.69 us -> 11.9 us  [on_device(): lax.ppermute(w_z, 'x', [(i, i ^ j) for i in range(x_size)])]
    ppermute x1, waiting for transfers between devices: 2.08 us -> 0.01 us  [on_device(): far_in = lax.ppermute(chip3, seq, to_far)]
    pallas_call x7 -> x8, Pallas kernels: 16.1 us -> 16.1 us  [call(): pl.pallas_call(kernel, out_shape=shapes[0] if one else shapes, in_specs=[...]
  transfers between devices with their start and end apart: 13 -> 13, of which waited for: 4 -> 3; matrix products, arithmetic and copies ran while one was open for 0% -> 0% of each run, Pallas kernels for 14% -> 14%
where the time goes in v3:
time: 85.3 us; the launch traced here: 84.3 us
  starting transfers between devices  57.7 us (68%)
  Pallas kernels  16.1 us (19%)
  waiting for transfers between devices  6.47 us (8%)
  local copies, waits for them, and re-layouts  3.77 us (4%)
    pallas_call x8, Pallas kernels, call(): pl.pallas_call(kernel, out_shape=shapes[0] if one else shapes, in_specs=[...  16.1 us
    ppermute x3, starting transfers between devices, on_device(): lax.ppermute(w_z, 'x', [(i, i ^ j) for i in range(x_size)])  11.9 us
    all_to_all x1, starting transfers between devices, to_all(): return lax.all_to_all(copies, axis, 0, 0, tiled=True)  11.3 us
    ppermute x1, starting transfers between devices, on_device(): from_three = lax.ppermute(attended, 'head', three)  9.95 us
    ppermute x1, starting transfers between devices, on_device(): side = lax.ppermute(side_own, seq, swap)  8.78 us
    ppermute x1, starting transfers between devices, on_device(): w_other = lax.ppermute(w_mine, seq, swap)  4.05 us
    unnamed x16, local copies, waits for them, and re-layouts  3.73 us
    ppermute x1, starting transfers between devices, on_device(): lower = lax.ppermute(from_three[half:], 'head', one)  3.36 us
  transfers between devices with their start and end apart: 13, of which 3 were waited for; matrix products, arithmetic and copies ran while one was open for 0% of the time, Pallas kernels for 14%

profile of v3, /device:TPU:1, one launch (start us, length us, event | category | flops | bytes accessed | tf_op | source)
XLA Modules:
  0.0 84.3 jit_solution(12304069679281160567)
XLA Ops:
  0.0 0.0 copy-start.1
  0.0 1.0 %copy-done.1 = bf16[512,512]{1,0:T(8,128)(2,1)S(1)} copy-done((bf16[512,512]{1,0:T(8,128)(2,1)S(1)}, bf16[512,512]{1,0:T(8,128)(2,1)}, u32[]{:S(2)}) %copy-start.1) | copy-done | bytes 524312
  1.0 0.0 copy-start.3
  1.0 1.0 %copy-done.3 = bf16[512,512]{1,0:T(8,128)(2,1)S(1)} copy-done((bf16[512,512]{1,0:T(8,128)(2,1)S(1)}, bf16[512,512]{1,0:T(8,128)(2,1)}, u32[]{:S(2)}) %copy-start.3) | copy-done | bytes 524312
  2.1 0.6 shard_map.46
  2.7 8.8 %collective-permute-start = (bf16[2,256,512]{2,1,0:T(8,128)(2,1)S(1)}, bf16[2,256,512]{2,1,0:T(8,128)(2,1)S(1)}, u32[]{:S(2)}, u32[]{:S(2)}) collective-permute-start(bf16[2,256,512]{2,1,0:T(8,128)(2,1)S(1)} %get-tuple-element.12), channel_id=1, source_target_pairs={{0,4},{4,0},{8,12},{12,8},{16,20},{20,16},{24,28},{28,24},{32,36},... | collective-permute-start | bytes 1572872 | tf_op jit(solution)/shard_map/ppermute | solution.py:324
  11.5 1.5 %collective-permute-done.pack_ref.side_ref = bf16[2,256,512]{2,1,0:T(8,128)(2,1)S(1)} collective-permute-done((bf16[2,256,512]{2,1,0:T(8,128)(2,1)S(1)}, bf16[2,256,512]{2,1,0:T(8,128)(2,1)S(1)}, u32[]{:S(2)}, u32[]{:S(2)}) %collective-permute-start) | collective-permute-done | bytes 524320 | tf_op jit(solution)/shard_map/ppermute | solution.py:324
  13.0 0.0 copy-start.5
  13.0 0.0 copy-start.7
  13.0 0.2 shard_map.47
  13.2 0.6 copy-done.5
  13.8 1.9 %collective-permute-start.1 = (bf16[2,320,512]{2,1,0:T(8,128)(2,1)S(1)}, bf16[2,320,512]{2,1,0:T(8,128)(2,1)S(1)}, u32[]{:S(2)}, u32[]{:S(2)}) collective-permute-start(bf16[2,320,512]{2,1,0:T(8,128)(2,1)S(1)} %get-tuple-element.16), channel_id=1, source_target_pairs={{4,8},{8,4},{12,16},{16,12},{20,24},{24,20},{28,32},{32,28},{36,40... | collective-permute-start | bytes 1966088 | tf_op jit(solution)/shard_map/ppermute | solution.py:339
  15.7 0.0 copy-done.7
  15.8 0.7 collective-permute-start.7
  16.4 1.4 %collective-permute-start.2 = (bf16[2,128,512]{2,1,0:T(8,128)(2,1)S(1)}, bf16[2,128,512]{2,1,0:T(8,128)(2,1)}, u32[]{:S(2)}, u32[]{:S(2)}) collective-permute-start(bf16[2,128,512]{2,1,0:T(8,128)(2,1)S(1)} %get-tuple-element.15.chip_ref.gate_hbm), channel_id=1, source_target_pairs={{0,12},{8,20},{12,0},{16,28},{20,8},{24,36},{28,16},{32,44},{36,24... | collective-permute-start | bytes 786440 | tf_op jit(solution)/shard_map/ppermute | solution.py:338
  17.8 0.0 collective-permute-done.7.value_hbm
  17.8 0.0 copy-start.2
  17.8 0.0 copy-start.4
  17.8 0.7 shard_map.51
  18.5 0.0 copy-start
  18.5 11.3 %all-to-all-start = ((bf16[16,16,512]{2,1,0:T(8,128)(2,1)}), bf16[16,16,512]{2,1,0:T(8,128)(2,1)S(1)}, u32[]{:S(2)}, u32[]{:S(2)}) async-start(bf16[16,16,512]{2,1,0:T(8,128)(2,1)} %shard_map.51), calls=%async_computation | async-start | bytes 524288 | tf_op jit(solution)/shard_map/all_to_all | solution.py:306
  29.8 0.0 collective-permute-done.2.far_ref
  29.8 0.0 collective-permute-done.1.near_ref
  29.8 0.0 copy-done.2
  29.8 0.0 copy-done.4
  29.8 0.0 copy-done
  29.9 0.0 copy-start.6
  29.9 1.0 %copy-done.6 = bf16[2,256,512]{2,1,0:T(8,128)(2,1)S(1)} copy-done((bf16[2,256,512]{2,1,0:T(8,128)(2,1)S(1)}, bf16[2,256,512]{2,1,0:T(8,128)(2,1)}, u32[]{:S(2)}) %copy-start.6) | copy-done | bytes 524312
  30.9 11.3 %shard_map.48.own_ref = bf16[512,512]{1,0:T(8,128)(2,1)} custom-call(bf16[512,512]{1,0:T(8,128)(2,1)S(1)} %copy-done, bf16[512,512]{1,0:T(8,128)(2,1)S(1)} %copy-done.2, bf16[512,512]{1,0:T(8,128)(2,1)S(1)} %copy-done.4, bf16[2,256,512]{2,1,0:T(8,128)(2,1)S(1)} %copy-done.6, bf16[2,128,512]{2,1,0:T(8,128)(2,1)S(1)} %get-tuple-element.15.chip_ref.gate_hbm, ...), custom_call_target="tpu_custom_call" | custom-call | flops 12099999744 | tf_op jit(solution)/shard_map/pallas_call | solution.py:284
  42.2 10.0 %collective-permute-start.4 = (bf16[512,512]{1,0:T(8,128)(2,1)}, bf16[512,512]{1,0:T(8,128)(2,1)S(1)}, u32[]{:S(2)}, u32[]{:S(2)}) collective-permute-start(bf16[512,512]{1,0:T(8,128)(2,1)} %shard_map.48.own_ref), channel_id=1, source_target_pairs={{0,3},{1,2},{2,1},{3,0},{4,7},{5,6},{6,5},{7,4},{8,11},{9,10},{10,... | collective-permute-start | bytes 1572872 | tf_op jit(solution)/shard_map/ppermute | solution.py:356
  52.2 2.5 %collective-permute-start.3 = (bf16[512,512]{1,0:T(8,128)(2,1)}, bf16[512,512]{1,0:T(8,128)(2,1)S(1)}, u32[]{:S(2)}, u32[]{:S(2)}) collective-permute-start(bf16[512,512]{1,0:T(8,128)(2,1)} %shard_map.48.own_ref), channel_id=1, source_target_pairs={{0,1},{1,0},{2,3},{3,2},{4,5},{5,4},{6,7},{7,6},{8,9},{9,8},{10,11... | collective-permute-start | bytes 1572872 | tf_op jit(solution)/shard_map/ppermute | solution.py:355
  54.7 0.0 all-to-all-done.a_hbm
  54.7 6.1 %collective-permute-start.10 = (bf16[16,16,512]{2,1,0:T(8,128)(2,1)S(1)}, bf16[16,16,512]{2,1,0:T(8,128)(2,1)S(1)}, u32[]{:S(2)}, u32[]{:S(2)}) collective-permute-start(bf16[16,16,512]{2,1,0:T(8,128)(2,1)S(1)} %all-to-all-done.a_hbm), channel_id=1, source_target_pairs={{0,384},{128,256},{256,128},{384,0},{1,385},{129,257},{257,129},{3... | collective-permute-start | bytes 786440 | tf_op jit(solution)/shard_map/ppermute | solution.py:359
  60.9 3.8 %collective-permute-start.9 = (bf16[16,16,512]{2,1,0:T(8,128)(2,1)S(1)}, bf16[16,16,512]{2,1,0:T(8,128)(2,1)S(1)}, u32[]{:S(2)}, u32[]{:S(2)}) collective-permute-start(bf16[16,16,512]{2,1,0:T(8,128)(2,1)S(1)} %all-to-all-done.a_hbm), channel_id=1, source_target_pairs={{0,256},{128,384},{256,0},{384,128},{1,257},{129,385},{257,1},{385... | collective-permute-start | bytes 786440 | tf_op jit(solution)/shard_map/ppermute | solution.py:359
  64.7 1.9 %collective-permute-start.8 = (bf16[16,16,512]{2,1,0:T(8,128)(2,1)S(1)}, bf16[16,16,512]{2,1,0:T(8,128)(2,1)S(1)}, u32[]{:S(2)}, u32[]{:S(2)}) collective-permute-start(bf16[16,16,512]{2,1,0:T(8,128)(2,1)S(1)} %all-to-all-done.a_hbm), channel_id=1, source_target_pairs={{0,128},{128,0},{256,384},{384,256},{1,129},{129,1},{257,385},{385... | collective-permute-start | bytes 786440 | tf_op jit(solution)/shard_map/ppermute | solution.py:359
  66.6 0.0 collective-permute-done.4.gate_3_hbm.three_ref
  66.7 3.4 %collective-permute-start.6 = (bf16[256,512]{1,0:T(8,128)(2,1)S(1)}, bf16[256,512]{1,0:T(8,128)(2,1)S(1)}, u32[]{:S(2)}, u32[]{:S(2)}) collective-permute-start(bf16[256,512]{1,0:T(8,128)(2,1)S(1)} %slice.9), channel_id=1, source_target_pairs={{0,1},{1,0},{2,3},{3,2},{4,5},{5,4},{6,7},{7,6},{8,9},{9,8},{10,11... | collective-permute-start | bytes 786440 | tf_op jit(solution)/shard_map/ppermute | solution.py:367
  70.1 0.0 collective-permute-done.3.gate_1_hbm.one_ref
  70.1 1.9 %collective-permute-start.5 = (bf16[256,512]{1,0:T(8,128)(2,1)S(1)}, bf16[256,512]{1,0:T(8,128)(2,1)S(1)}, u32[]{:S(2)}, u32[]{:S(2)}) collective-permute-start(bf16[256,512]{1,0:T(8,128)(2,1)S(1)} %slice.8), channel_id=1, source_target_pairs={{0,3},{1,2},{2,1},{3,0},{4,7},{5,6},{6,5},{7,4},{8,11},{9,10},{10,... | collective-permute-start | bytes 786440 | tf_op jit(solution)/shard_map/ppermute | solution.py:366
  72.0 0.0 collective-permute-done.10.d_hbm
  72.0 0.0 collective-permute-done.9.c_hbm
  72.0 2.7 %collective-permute-done.8.b_hbm = bf16[16,16,512]{2,1,0:T(8,128)(2,1)S(1)} collective-permute-done((bf16[16,16,512]{2,1,0:T(8,128)(2,1)S(1)}, bf16[16,16,512]{2,1,0:T(8,128)(2,1)S(1)}, u32[]{:S(2)}, u32[]{:S(2)}) %collective-permute-start.8) | collective-permute-done | bytes 262176 | tf_op jit(solution)/shard_map/ppermute | solution.py:359
  74.7 0.1 shard_map.52.mine_ref
  74.9 4.1 %collective-permute-start.11 = (bf16[4,16,16,512]{3,2,1,0:T(8,128)(2,1)S(1)}, bf16[4,16,16,512]{3,2,1,0:T(8,128)(2,1)S(1)}, u32[]{:S(2)}, u32[]{:S(2)}) collective-permute-start(bf16[4,16,16,512]{3,2,1,0:T(8,128)(2,1)S(1)} %shard_map.52.mine_ref), channel_id=1, source_target_pairs={{0,4},{4,0},{8,12},{12,8},{16,20},{20,16},{24,28},{28,24},{32,36},... | collective-permute-start | bytes 3145736 | tf_op jit(solution)/shard_map/ppermute | solution.py:364
  78.9 0.0 collective-permute-done.6.lower_hbm
  78.9 0.0 collective-permute-done.5.upper_hbm
  78.9 2.2 %collective-permute-done.11.other_ref = bf16[4,16,16,512]{3,2,1,0:T(8,128)(2,1)S(1)} collective-permute-done((bf16[4,16,16,512]{3,2,1,0:T(8,128)(2,1)S(1)}, bf16[4,16,16,512]{3,2,1,0:T(8,128)(2,1)S(1)}, u32[]{:S(2)}, u32[]{:S(2)}) %collective-permute-start.11) | collective-permute-done | bytes 1048608 | tf_op jit(solution)/shard_map/ppermute | solution.py:364
  81.2 3.1 %shard_map.53 = bf16[512,512]{1,0:T(8,128)(2,1)} custom-call(bf16[512,512]{1,0:T(8,128)(2,1)} %shard_map.48.own_ref, bf16[512,512]{1,0:T(8,128)(2,1)S(1)} %collective-permute-done.3.gate_1_hbm.one_ref, bf16[512,512]{1,0:T(8,128)(2,1)S(1)} %collective-permute-done.4.gate_3_hbm.three_ref, bf16[256,512]{1,0:T(8,128)(2,1)S(1)} %get-tuple-element.17.upper_ref, ...), custom_call_target="tpu_custom_call" | custom-call | flops 3300000000 | tf_op jit(solution)/shard_map/pallas_call | solution.py:284
  (4 shorter events, 0.0 us)
Async XLA Ops:
  0.0 1.0 %copy-start.1 = (bf16[512,512]{1,0:T(8,128)(2,1)S(1)}, bf16[512,512]{1,0:T(8,128)(2,1)}, u32[]{:S(2)}) copy-start(bf16[512,512]{1,0:T(8,128)(2,1)} %k_ref.1) | copy-start | bytes 1572868
  1.0 1.0 %copy-start.3 = (bf16[512,512]{1,0:T(8,128)(2,1)S(1)}, bf16[512,512]{1,0:T(8,128)(2,1)}, u32[]{:S(2)}) copy-start(bf16[512,512]{1,0:T(8,128)(2,1)} %v_ref.1) | copy-start | bytes 1572868
  2.7 10.3 %collective-permute-start = (bf16[2,256,512]{2,1,0:T(8,128)(2,1)S(1)}, bf16[2,256,512]{2,1,0:T(8,128)(2,1)S(1)}, u32[]{:S(2)}, u32[]{:S(2)}) collective-permute-start(bf16[2,256,512]{2,1,0:T(8,128)(2,1)S(1)} %get-tuple-element.12), channel_id=1, source_target_pairs={{0,4},{4,0},{8,12},{12,8},{16,20},{20,16},{24,28},{28,24},{32,36},... | collective-permute-start | bytes 1572872 | tf_op jit(solution)/shard_map/ppermute | solution.py:324
  13.0 0.8 copy-start.5
  13.0 2.7 %copy-start.7 = (bf16[512,16]{0,1:T(8,128)(2,1)S(1)}, bf16[512,16]{0,1:T(8,128)(2,1)}, u32[]{:S(2)}) copy-start(bf16[512,16]{0,1:T(8,128)(2,1)} %param.7) | copy-start | bytes 49156
  13.8 16.0 %collective-permute-start.1 = (bf16[2,320,512]{2,1,0:T(8,128)(2,1)S(1)}, bf16[2,320,512]{2,1,0:T(8,128)(2,1)S(1)}, u32[]{:S(2)}, u32[]{:S(2)}) collective-permute-start(bf16[2,320,512]{2,1,0:T(8,128)(2,1)S(1)} %get-tuple-element.16), channel_id=1, source_target_pairs={{4,8},{8,4},{12,16},{16,12},{20,24},{24,20},{28,32},{32,28},{36,40... | collective-permute-start | bytes 1966088 | tf_op jit(solution)/shard_map/ppermute | solution.py:339
  15.8 2.0 %collective-permute-start.7 = (bf16[16,512]{1,0:T(8,128)(2,1)S(1)}, bf16[16,512]{1,0:T(8,128)(2,1)S(1)}, u32[]{:S(2)}, u32[]{:S(2)}) collective-permute-start(bf16[16,512]{1,0:T(8,128)(2,1)S(1)} %bitcast.1), channel_id=1, source_target_pairs={{0,0},{1,128},{2,256},{3,384},{128,1},{129,129},{130,257},{131,385... | collective-permute-start | bytes 49160 | tf_op jit(solution)/shard_map/ppermute | solution.py:326
  16.4 13.4 %collective-permute-start.2 = (bf16[2,128,512]{2,1,0:T(8,128)(2,1)S(1)}, bf16[2,128,512]{2,1,0:T(8,128)(2,1)}, u32[]{:S(2)}, u32[]{:S(2)}) collective-permute-start(bf16[2,128,512]{2,1,0:T(8,128)(2,1)S(1)} %get-tuple-element.15.chip_ref.gate_hbm), channel_id=1, source_target_pairs={{0,12},{8,20},{12,0},{16,28},{20,8},{24,36},{28,16},{32,44},{36,24... | collective-permute-start | bytes 786440 | tf_op jit(solution)/shard_map/ppermute | solution.py:338
  17.8 12.0 %copy-start.2 = (bf16[512,512]{1,0:T(8,128)(2,1)S(1)}, bf16[512,512]{1,0:T(8,128)(2,1)}, u32[]{:S(2)}) copy-start(bf16[512,512]{1,0:T(8,128)(2,1)} %k_ref.1) | copy-start | bytes 1572868
  17.8 12.0 %copy-start.4 = (bf16[512,512]{1,0:T(8,128)(2,1)S(1)}, bf16[512,512]{1,0:T(8,128)(2,1)}, u32[]{:S(2)}) copy-start(bf16[512,512]{1,0:T(8,128)(2,1)} %v_ref.1) | copy-start | bytes 1572868
  18.5 11.3 %copy-start = (bf16[512,512]{1,0:T(8,128)(2,1)S(1)}, bf16[512,512]{1,0:T(8,128)(2,1)}, u32[]{:S(2)}) copy-start(bf16[512,512]{1,0:T(8,128)(2,1)} %q_ref.1) | copy-start | bytes 1572868
  18.5 36.2 %all-to-all-start = ((bf16[16,16,512]{2,1,0:T(8,128)(2,1)}), bf16[16,16,512]{2,1,0:T(8,128)(2,1)S(1)}, u32[]{:S(2)}, u32[]{:S(2)}) async-start(bf16[16,16,512]{2,1,0:T(8,128)(2,1)} %shard_map.51), calls=%async_computation | async-start | bytes 524288 | tf_op jit(solution)/shard_map/all_to_all | solution.py:306
  29.9 1.0 %copy-start.6 = (bf16[2,256,512]{2,1,0:T(8,128)(2,1)S(1)}, bf16[2,256,512]{2,1,0:T(8,128)(2,1)}, u32[]{:S(2)}) copy-start(bf16[2,256,512]{2,1,0:T(8,128)(2,1)} %copy-done.5) | copy-start | bytes 1572868
  42.2 24.4 %collective-permute-start.4 = (bf16[512,512]{1,0:T(8,128)(2,1)}, bf16[512,512]{1,0:T(8,128)(2,1)S(1)}, u32[]{:S(2)}, u32[]{:S(2)}) collective-permute-start(bf16[512,512]{1,0:T(8,128)(2,1)} %shard_map.48.own_ref), channel_id=1, source_target_pairs={{0,3},{1,2},{2,1},{3,0},{4,7},{5,6},{6,5},{7,4},{8,11},{9,10},{10,... | collective-permute-start | bytes 1572872 | tf_op jit(solution)/shard_map/ppermute | solution.py:356
  52.2 17.9 %collective-permute-start.3 = (bf16[512,512]{1,0:T(8,128)(2,1)}, bf16[512,512]{1,0:T(8,128)(2,1)S(1)}, u32[]{:S(2)}, u32[]{:S(2)}) collective-permute-start(bf16[512,512]{1,0:T(8,128)(2,1)} %shard_map.48.own_ref), channel_id=1, source_target_pairs={{0,1},{1,0},{2,3},{3,2},{4,5},{5,4},{6,7},{7,6},{8,9},{9,8},{10,11... | collective-permute-start | bytes 1572872 | tf_op jit(solution)/shard_map/ppermute | solution.py:355
  54.7 17.3 %collective-permute-start.10 = (bf16[16,16,512]{2,1,0:T(8,128)(2,1)S(1)}, bf16[16,16,512]{2,1,0:T(8,128)(2,1)S(1)}, u32[]{:S(2)}, u32[]{:S(2)}) collective-permute-start(bf16[16,16,512]{2,1,0:T(8,128)(2,1)S(1)} %all-to-all-done.a_hbm), channel_id=1, source_target_pairs={{0,384},{128,256},{256,128},{384,0},{1,385},{129,257},{257,129},{3... | collective-permute-start | bytes 786440 | tf_op jit(solution)/shard_map/ppermute | solution.py:359
  60.9 11.1 %collective-permute-start.9 = (bf16[16,16,512]{2,1,0:T(8,128)(2,1)S(1)}, bf16[16,16,512]{2,1,0:T(8,128)(2,1)S(1)}, u32[]{:S(2)}, u32[]{:S(2)}) collective-permute-start(bf16[16,16,512]{2,1,0:T(8,128)(2,1)S(1)} %all-to-all-done.a_hbm), channel_id=1, source_target_pairs={{0,256},{128,384},{256,0},{384,128},{1,257},{129,385},{257,1},{385... | collective-permute-start | bytes 786440 | tf_op jit(solution)/shard_map/ppermute | solution.py:359
  64.7 10.0 %collective-permute-start.8 = (bf16[16,16,512]{2,1,0:T(8,128)(2,1)S(1)}, bf16[16,16,512]{2,1,0:T(8,128)(2,1)S(1)}, u32[]{:S(2)}, u32[]{:S(2)}) collective-permute-start(bf16[16,16,512]{2,1,0:T(8,128)(2,1)S(1)} %all-to-all-done.a_hbm), channel_id=1, source_target_pairs={{0,128},{128,0},{256,384},{384,256},{1,129},{129,1},{257,385},{385... | collective-permute-start | bytes 786440 | tf_op jit(solution)/shard_map/ppermute | solution.py:359
  66.7 12.2 %collective-permute-start.6 = (bf16[256,512]{1,0:T(8,128)(2,1)S(1)}, bf16[256,512]{1,0:T(8,128)(2,1)S(1)}, u32[]{:S(2)}, u32[]{:S(2)}) collective-permute-start(bf16[256,512]{1,0:T(8,128)(2,1)S(1)} %slice.9), channel_id=1, source_target_pairs={{0,1},{1,0},{2,3},{3,2},{4,5},{5,4},{6,7},{7,6},{8,9},{9,8},{10,11... | collective-permute-start | bytes 786440 | tf_op jit(solution)/shard_map/ppermute | solution.py:367
  70.1 8.8 %collective-permute-start.5 = (bf16[256,512]{1,0:T(8,128)(2,1)S(1)}, bf16[256,512]{1,0:T(8,128)(2,1)S(1)}, u32[]{:S(2)}, u32[]{:S(2)}) collective-permute-start(bf16[256,512]{1,0:T(8,128)(2,1)S(1)} %slice.8), channel_id=1, source_target_pairs={{0,3},{1,2},{2,1},{3,0},{4,7},{5,6},{6,5},{7,4},{8,11},{9,10},{10,... | collective-permute-start | bytes 786440 | tf_op jit(solution)/shard_map/ppermute | solution.py:366
  74.9 6.3 %collective-permute-start.11 = (bf16[4,16,16,512]{3,2,1,0:T(8,128)(2,1)S(1)}, bf16[4,16,16,512]{3,2,1,0:T(8,128)(2,1)S(1)}, u32[]{:S(2)}, u32[]{:S(2)}) collective-permute-start(bf16[4,16,16,512]{3,2,1,0:T(8,128)(2,1)S(1)} %shard_map.52.mine_ref), channel_id=1, source_target_pairs={{0,4},{4,0},{8,12},{12,8},{16,20},{20,16},{24,28},{28,24},{32,36},... | collective-permute-start | bytes 3145736 | tf_op jit(solution)/shard_map/ppermute | solution.py:364

commit v4 on v3

--- a/solution.py
+++ b/solution.py
@@ -153,8 +153,8 @@
         scores = jnp.concatenate([scores[:, :128] + bias_left, scores[:, 128:]], axis=1)
     if bias_right is not None:
         scores = jnp.concatenate([scores[:, :256], scores[:, 256:] + bias_right], axis=1)
-    top = jnp.max(scores, axis=1, keepdims=True)
-    probs = jnp.exp2((scores - top) * SCALE2).astype(BF16)
+    top = jnp.broadcast_to(jnp.max(scores, axis=1, keepdims=True), (scores.shape[0], 128))
+    probs = jnp.exp2((scores - jnp.concatenate([top] * 3, axis=1)) * SCALE2).astype(BF16)
     wide = jnp.concatenate(values, axis=0)
     wide = jnp.concatenate([wide, jnp.ones_like(wide)], axis=1)
     return top, dot(probs, wide)
@@ -167,6 +167,8 @@
     higher = fine_top >= top
     fine_factor = jnp.where(higher, 1.0, fall)
     factor = jnp.where(higher, fall, 1.0)
+    fine_factor = jnp.concatenate([fine_factor] * 2, axis=1)
+    factor = jnp.concatenate([factor] * 2, axis=1)
     return jnp.maximum(fine_top, top), fine_sums * fine_factor + sums * factor
 
 

time: 85.3 us -> 85.3 us (level)
  no operation moved by 1% of the time
where the time goes in v4:
time: 85.3 us; the launch traced here: 84.3 us
  starting transfers between devices  57.7 us (68%)
  Pallas kernels  16.1 us (19%)
  waiting for transfers between devices  6.47 us (8%)
  local copies, waits for them, and re-layouts  3.77 us (4%)
    pallas_call x8, Pallas kernels, call(): pl.pallas_call(kernel, out_shape=shapes[0] if one else shapes, in_specs=[...  16.1 us
    ppermute x3, starting transfers between devices, on_device(): lax.ppermute(w_z, 'x', [(i, i ^ j) for i in range(x_size)])  11.9 us
    all_to_all x1, starting transfers between devices, to_all(): return lax.all_to_all(copies, axis, 0, 0, tiled=True)  11.3 us
    ppermute x1, starting transfers between devices, on_device(): from_three = lax.ppermute(attended, 'head', three)  9.95 us
    ppermute x1, starting transfers between devices, on_device(): side = lax.ppermute(side_own, seq, swap)  8.78 us
    ppermute x1, starting transfers between devices, on_device(): w_other = lax.ppermute(w_mine, seq, swap)  4.05 us
    unnamed x16, local copies, waits for them, and re-layouts  3.73 us
    ppermute x1, starting transfers between devices, on_device(): lower = lax.ppermute(from_three[half:], 'head', one)  3.36 us
  transfers between devices with their start and end apart: 13, of which 3 were waited for; matrix products, arithmetic and copies ran while one was open for 0% of the time, Pallas kernels for 14%

profile of v4, /device:TPU:1, one launch (start us, length us, event | category | flops | bytes accessed | tf_op | source)
XLA Modules:
  0.0 84.3 jit_solution(3180108258388847417)
XLA Ops:
  0.0 0.0 copy-start.1
  0.0 1.0 %copy-done.1 = bf16[512,512]{1,0:T(8,128)(2,1)S(1)} copy-done((bf16[512,512]{1,0:T(8,128)(2,1)S(1)}, bf16[512,512]{1,0:T(8,128)(2,1)}, u32[]{:S(2)}) %copy-start.1) | copy-done | bytes 524312
  1.0 0.0 copy-start.3
  1.0 1.0 %copy-done.3 = bf16[512,512]{1,0:T(8,128)(2,1)S(1)} copy-done((bf16[512,512]{1,0:T(8,128)(2,1)S(1)}, bf16[512,512]{1,0:T(8,128)(2,1)}, u32[]{:S(2)}) %copy-start.3) | copy-done | bytes 524312
  2.1 0.6 shard_map.46
  2.7 8.8 %collective-permute-start = (bf16[2,256,512]{2,1,0:T(8,128)(2,1)S(1)}, bf16[2,256,512]{2,1,0:T(8,128)(2,1)S(1)}, u32[]{:S(2)}, u32[]{:S(2)}) collective-permute-start(bf16[2,256,512]{2,1,0:T(8,128)(2,1)S(1)} %get-tuple-element.12), channel_id=1, source_target_pairs={{0,4},{4,0},{8,12},{12,8},{16,20},{20,16},{24,28},{28,24},{32,36},... | collective-permute-start | bytes 1572872 | tf_op jit(solution)/shard_map/ppermute | solution.py:326
  11.5 1.5 %collective-permute-done.pack_ref.side_ref = bf16[2,256,512]{2,1,0:T(8,128)(2,1)S(1)} collective-permute-done((bf16[2,256,512]{2,1,0:T(8,128)(2,1)S(1)}, bf16[2,256,512]{2,1,0:T(8,128)(2,1)S(1)}, u32[]{:S(2)}, u32[]{:S(2)}) %collective-permute-start) | collective-permute-done | bytes 524320 | tf_op jit(solution)/shard_map/ppermute | solution.py:326
  13.0 0.0 copy-start.5
  13.0 0.0 copy-start.7
  13.0 0.2 shard_map.47
  13.2 0.6 copy-done.5
  13.8 1.9 %collective-permute-start.1 = (bf16[2,320,512]{2,1,0:T(8,128)(2,1)S(1)}, bf16[2,320,512]{2,1,0:T(8,128)(2,1)S(1)}, u32[]{:S(2)}, u32[]{:S(2)}) collective-permute-start(bf16[2,320,512]{2,1,0:T(8,128)(2,1)S(1)} %get-tuple-element.16), channel_id=1, source_target_pairs={{4,8},{8,4},{12,16},{16,12},{20,24},{24,20},{28,32},{32,28},{36,40... | collective-permute-start | bytes 1966088 | tf_op jit(solution)/shard_map/ppermute | solution.py:341
  15.7 0.0 copy-done.7
  15.8 0.7 collective-permute-start.7
  16.4 1.4 %collective-permute-start.2 = (bf16[2,128,512]{2,1,0:T(8,128)(2,1)S(1)}, bf16[2,128,512]{2,1,0:T(8,128)(2,1)}, u32[]{:S(2)}, u32[]{:S(2)}) collective-permute-start(bf16[2,128,512]{2,1,0:T(8,128)(2,1)S(1)} %get-tuple-element.15.chip_ref.gate_hbm), channel_id=1, source_target_pairs={{0,12},{8,20},{12,0},{16,28},{20,8},{24,36},{28,16},{32,44},{36,24... | collective-permute-start | bytes 786440 | tf_op jit(solution)/shard_map/ppermute | solution.py:340
  17.8 0.0 collective-permute-done.7.value_hbm
  17.8 0.0 copy-start.2
  17.8 0.0 copy-start.4
  17.8 0.7 shard_map.51
  18.5 0.0 copy-start
  18.5 11.3 %all-to-all-start = ((bf16[16,16,512]{2,1,0:T(8,128)(2,1)}), bf16[16,16,512]{2,1,0:T(8,128)(2,1)S(1)}, u32[]{:S(2)}, u32[]{:S(2)}) async-start(bf16[16,16,512]{2,1,0:T(8,128)(2,1)} %shard_map.51), calls=%async_computation | async-start | bytes 524288 | tf_op jit(solution)/shard_map/all_to_all | solution.py:308
  29.8 0.0 collective-permute-done.2.far_ref
  29.8 0.0 collective-permute-done.1.near_ref
  29.8 0.0 copy-done.2
  29.8 0.0 copy-done.4
  29.8 0.0 copy-done
  29.9 0.0 copy-start.6
  29.9 1.0 %copy-done.6 = bf16[2,256,512]{2,1,0:T(8,128)(2,1)S(1)} copy-done((bf16[2,256,512]{2,1,0:T(8,128)(2,1)S(1)}, bf16[2,256,512]{2,1,0:T(8,128)(2,1)}, u32[]{:S(2)}) %copy-start.6) | copy-done | bytes 524312
  30.9 11.3 %shard_map.48.own_ref = bf16[512,512]{1,0:T(8,128)(2,1)} custom-call(bf16[512,512]{1,0:T(8,128)(2,1)S(1)} %copy-done, bf16[512,512]{1,0:T(8,128)(2,1)S(1)} %copy-done.2, bf16[512,512]{1,0:T(8,128)(2,1)S(1)} %copy-done.4, bf16[2,256,512]{2,1,0:T(8,128)(2,1)S(1)} %copy-done.6, bf16[2,128,512]{2,1,0:T(8,128)(2,1)S(1)} %get-tuple-element.15.chip_ref.gate_hbm, ...), custom_call_target="tpu_custom_call" | custom-call | flops 12099999744 | tf_op jit(solution)/shard_map/pallas_call | solution.py:286
  42.2 10.0 %collective-permute-start.4 = (bf16[512,512]{1,0:T(8,128)(2,1)}, bf16[512,512]{1,0:T(8,128)(2,1)S(1)}, u32[]{:S(2)}, u32[]{:S(2)}) collective-permute-start(bf16[512,512]{1,0:T(8,128)(2,1)} %shard_map.48.own_ref), channel_id=1, source_target_pairs={{0,3},{1,2},{2,1},{3,0},{4,7},{5,6},{6,5},{7,4},{8,11},{9,10},{10,... | collective-permute-start | bytes 1572872 | tf_op jit(solution)/shard_map/ppermute | solution.py:358
  52.2 2.5 %collective-permute-start.3 = (bf16[512,512]{1,0:T(8,128)(2,1)}, bf16[512,512]{1,0:T(8,128)(2,1)S(1)}, u32[]{:S(2)}, u32[]{:S(2)}) collective-permute-start(bf16[512,512]{1,0:T(8,128)(2,1)} %shard_map.48.own_ref), channel_id=1, source_target_pairs={{0,1},{1,0},{2,3},{3,2},{4,5},{5,4},{6,7},{7,6},{8,9},{9,8},{10,11... | collective-permute-start | bytes 1572872 | tf_op jit(solution)/shard_map/ppermute | solution.py:357
  54.7 0.0 all-to-all-done.a_hbm
  54.7 6.1 %collective-permute-start.10 = (bf16[16,16,512]{2,1,0:T(8,128)(2,1)S(1)}, bf16[16,16,512]{2,1,0:T(8,128)(2,1)S(1)}, u32[]{:S(2)}, u32[]{:S(2)}) collective-permute-start(bf16[16,16,512]{2,1,0:T(8,128)(2,1)S(1)} %all-to-all-done.a_hbm), channel_id=1, source_target_pairs={{0,384},{128,256},{256,128},{384,0},{1,385},{129,257},{257,129},{3... | collective-permute-start | bytes 786440 | tf_op jit(solution)/shard_map/ppermute | solution.py:361
  60.9 3.8 %collective-permute-start.9 = (bf16[16,16,512]{2,1,0:T(8,128)(2,1)S(1)}, bf16[16,16,512]{2,1,0:T(8,128)(2,1)S(1)}, u32[]{:S(2)}, u32[]{:S(2)}) collective-permute-start(bf16[16,16,512]{2,1,0:T(8,128)(2,1)S(1)} %all-to-all-done.a_hbm), channel_id=1, source_target_pairs={{0,256},{128,384},{256,0},{384,128},{1,257},{129,385},{257,1},{385... | collective-permute-start | bytes 786440 | tf_op jit(solution)/shard_map/ppermute | solution.py:361
  64.7 1.9 %collective-permute-start.8 = (bf16[16,16,512]{2,1,0:T(8,128)(2,1)S(1)}, bf16[16,16,512]{2,1,0:T(8,128)(2,1)S(1)}, u32[]{:S(2)}, u32[]{:S(2)}) collective-permute-start(bf16[16,16,512]{2,1,0:T(8,128)(2,1)S(1)} %all-to-all-done.a_hbm), channel_id=1, source_target_pairs={{0,128},{128,0},{256,384},{384,256},{1,129},{129,1},{257,385},{385... | collective-permute-start | bytes 786440 | tf_op jit(solution)/shard_map/ppermute | solution.py:361
  66.6 0.0 collective-permute-done.4.gate_3_hbm.three_ref
  66.7 3.4 %collective-permute-start.6 = (bf16[256,512]{1,0:T(8,128)(2,1)S(1)}, bf16[256,512]{1,0:T(8,128)(2,1)S(1)}, u32[]{:S(2)}, u32[]{:S(2)}) collective-permute-start(bf16[256,512]{1,0:T(8,128)(2,1)S(1)} %slice.9), channel_id=1, source_target_pairs={{0,1},{1,0},{2,3},{3,2},{4,5},{5,4},{6,7},{7,6},{8,9},{9,8},{10,11... | collective-permute-start | bytes 786440 | tf_op jit(solution)/shard_map/ppermute | solution.py:369
  70.0 0.0 collective-permute-done.3.gate_1_hbm.one_ref
  70.1 1.9 %collective-permute-start.5 = (bf16[256,512]{1,0:T(8,128)(2,1)S(1)}, bf16[256,512]{1,0:T(8,128)(2,1)S(1)}, u32[]{:S(2)}, u32[]{:S(2)}) collective-permute-start(bf16[256,512]{1,0:T(8,128)(2,1)S(1)} %slice.8), channel_id=1, source_target_pairs={{0,3},{1,2},{2,1},{3,0},{4,7},{5,6},{6,5},{7,4},{8,11},{9,10},{10,... | collective-permute-start | bytes 786440 | tf_op jit(solution)/shard_map/ppermute | solution.py:368
  72.0 0.0 collective-permute-done.10.d_hbm
  72.0 0.0 collective-permute-done.9.c_hbm
  72.0 2.7 %collective-permute-done.8.b_hbm = bf16[16,16,512]{2,1,0:T(8,128)(2,1)S(1)} collective-permute-done((bf16[16,16,512]{2,1,0:T(8,128)(2,1)S(1)}, bf16[16,16,512]{2,1,0:T(8,128)(2,1)S(1)}, u32[]{:S(2)}, u32[]{:S(2)}) %collective-permute-start.8) | collective-permute-done | bytes 262176 | tf_op jit(solution)/shard_map/ppermute | solution.py:361
  74.7 0.1 shard_map.52.mine_ref
  74.8 4.1 %collective-permute-start.11 = (bf16[4,16,16,512]{3,2,1,0:T(8,128)(2,1)S(1)}, bf16[4,16,16,512]{3,2,1,0:T(8,128)(2,1)S(1)}, u32[]{:S(2)}, u32[]{:S(2)}) collective-permute-start(bf16[4,16,16,512]{3,2,1,0:T(8,128)(2,1)S(1)} %shard_map.52.mine_ref), channel_id=1, source_target_pairs={{0,4},{4,0},{8,12},{12,8},{16,20},{20,16},{24,28},{28,24},{32,36},... | collective-permute-start | bytes 3145736 | tf_op jit(solution)/shard_map/ppermute | solution.py:366
  78.9 0.0 collective-permute-done.6.lower_hbm
  78.9 0.0 collective-permute-done.5.upper_hbm
  78.9 2.2 %collective-permute-done.11.other_ref = bf16[4,16,16,512]{3,2,1,0:T(8,128)(2,1)S(1)} collective-permute-done((bf16[4,16,16,512]{3,2,1,0:T(8,128)(2,1)S(1)}, bf16[4,16,16,512]{3,2,1,0:T(8,128)(2,1)S(1)}, u32[]{:S(2)}, u32[]{:S(2)}) %collective-permute-start.11) | collective-permute-done | bytes 1048608 | tf_op jit(solution)/shard_map/ppermute | solution.py:366
  81.1 3.1 %shard_map.53 = bf16[512,512]{1,0:T(8,128)(2,1)} custom-call(bf16[512,512]{1,0:T(8,128)(2,1)} %shard_map.48.own_ref, bf16[512,512]{1,0:T(8,128)(2,1)S(1)} %collective-permute-done.3.gate_1_hbm.one_ref, bf16[512,512]{1,0:T(8,128)(2,1)S(1)} %collective-permute-done.4.gate_3_hbm.three_ref, bf16[256,512]{1,0:T(8,128)(2,1)S(1)} %get-tuple-element.17.upper_ref, ...), custom_call_target="tpu_custom_call" | custom-call | flops 3300000000 | tf_op jit(solution)/shard_map/pallas_call | solution.py:286
  (4 shorter events, 0.0 us)
Async XLA Ops:
  0.0 1.0 %copy-start.1 = (bf16[512,512]{1,0:T(8,128)(2,1)S(1)}, bf16[512,512]{1,0:T(8,128)(2,1)}, u32[]{:S(2)}) copy-start(bf16[512,512]{1,0:T(8,128)(2,1)} %k_ref.1) | copy-start | bytes 1572868
  1.0 1.0 %copy-start.3 = (bf16[512,512]{1,0:T(8,128)(2,1)S(1)}, bf16[512,512]{1,0:T(8,128)(2,1)}, u32[]{:S(2)}) copy-start(bf16[512,512]{1,0:T(8,128)(2,1)} %v_ref.1) | copy-start | bytes 1572868
  2.7 10.3 %collective-permute-start = (bf16[2,256,512]{2,1,0:T(8,128)(2,1)S(1)}, bf16[2,256,512]{2,1,0:T(8,128)(2,1)S(1)}, u32[]{:S(2)}, u32[]{:S(2)}) collective-permute-start(bf16[2,256,512]{2,1,0:T(8,128)(2,1)S(1)} %get-tuple-element.12), channel_id=1, source_target_pairs={{0,4},{4,0},{8,12},{12,8},{16,20},{20,16},{24,28},{28,24},{32,36},... | collective-permute-start | bytes 1572872 | tf_op jit(solution)/shard_map/ppermute | solution.py:326
  13.0 0.8 copy-start.5
  13.0 2.7 %copy-start.7 = (bf16[512,16]{0,1:T(8,128)(2,1)S(1)}, bf16[512,16]{0,1:T(8,128)(2,1)}, u32[]{:S(2)}) copy-start(bf16[512,16]{0,1:T(8,128)(2,1)} %param.7) | copy-start | bytes 49156
  13.8 16.0 %collective-permute-start.1 = (bf16[2,320,512]{2,1,0:T(8,128)(2,1)S(1)}, bf16[2,320,512]{2,1,0:T(8,128)(2,1)S(1)}, u32[]{:S(2)}, u32[]{:S(2)}) collective-permute-start(bf16[2,320,512]{2,1,0:T(8,128)(2,1)S(1)} %get-tuple-element.16), channel_id=1, source_target_pairs={{4,8},{8,4},{12,16},{16,12},{20,24},{24,20},{28,32},{32,28},{36,40... | collective-permute-start | bytes 1966088 | tf_op jit(solution)/shard_map/ppermute | solution.py:341
  15.8 2.0 %collective-permute-start.7 = (bf16[16,512]{1,0:T(8,128)(2,1)S(1)}, bf16[16,512]{1,0:T(8,128)(2,1)S(1)}, u32[]{:S(2)}, u32[]{:S(2)}) collective-permute-start(bf16[16,512]{1,0:T(8,128)(2,1)S(1)} %bitcast.1), channel_id=1, source_target_pairs={{0,0},{1,128},{2,256},{3,384},{128,1},{129,129},{130,257},{131,385... | collective-permute-start | bytes 49160 | tf_op jit(solution)/shard_map/ppermute | solution.py:328
  16.4 13.4 %collective-permute-start.2 = (bf16[2,128,512]{2,1,0:T(8,128)(2,1)S(1)}, bf16[2,128,512]{2,1,0:T(8,128)(2,1)}, u32[]{:S(2)}, u32[]{:S(2)}) collective-permute-start(bf16[2,128,512]{2,1,0:T(8,128)(2,1)S(1)} %get-tuple-element.15.chip_ref.gate_hbm), channel_id=1, source_target_pairs={{0,12},{8,20},{12,0},{16,28},{20,8},{24,36},{28,16},{32,44},{36,24... | collective-permute-start | bytes 786440 | tf_op jit(solution)/shard_map/ppermute | solution.py:340
  17.8 12.0 %copy-start.2 = (bf16[512,512]{1,0:T(8,128)(2,1)S(1)}, bf16[512,512]{1,0:T(8,128)(2,1)}, u32[]{:S(2)}) copy-start(bf16[512,512]{1,0:T(8,128)(2,1)} %k_ref.1) | copy-start | bytes 1572868
  17.8 12.0 %copy-start.4 = (bf16[512,512]{1,0:T(8,128)(2,1)S(1)}, bf16[512,512]{1,0:T(8,128)(2,1)}, u32[]{:S(2)}) copy-start(bf16[512,512]{1,0:T(8,128)(2,1)} %v_ref.1) | copy-start | bytes 1572868
  18.5 11.3 %copy-start = (bf16[512,512]{1,0:T(8,128)(2,1)S(1)}, bf16[512,512]{1,0:T(8,128)(2,1)}, u32[]{:S(2)}) copy-start(bf16[512,512]{1,0:T(8,128)(2,1)} %q_ref.1) | copy-start | bytes 1572868
  18.5 36.2 %all-to-all-start = ((bf16[16,16,512]{2,1,0:T(8,128)(2,1)}), bf16[16,16,512]{2,1,0:T(8,128)(2,1)S(1)}, u32[]{:S(2)}, u32[]{:S(2)}) async-start(bf16[16,16,512]{2,1,0:T(8,128)(2,1)} %shard_map.51), calls=%async_computation | async-start | bytes 524288 | tf_op jit(solution)/shard_map/all_to_all | solution.py:308
  29.9 1.0 %copy-start.6 = (bf16[2,256,512]{2,1,0:T(8,128)(2,1)S(1)}, bf16[2,256,512]{2,1,0:T(8,128)(2,1)}, u32[]{:S(2)}) copy-start(bf16[2,256,512]{2,1,0:T(8,128)(2,1)} %copy-done.5) | copy-start | bytes 1572868
  42.2 24.4 %collective-permute-start.4 = (bf16[512,512]{1,0:T(8,128)(2,1)}, bf16[512,512]{1,0:T(8,128)(2,1)S(1)}, u32[]{:S(2)}, u32[]{:S(2)}) collective-permute-start(bf16[512,512]{1,0:T(8,128)(2,1)} %shard_map.48.own_ref), channel_id=1, source_target_pairs={{0,3},{1,2},{2,1},{3,0},{4,7},{5,6},{6,5},{7,4},{8,11},{9,10},{10,... | collective-permute-start | bytes 1572872 | tf_op jit(solution)/shard_map/ppermute | solution.py:358
  52.2 17.9 %collective-permute-start.3 = (bf16[512,512]{1,0:T(8,128)(2,1)}, bf16[512,512]{1,0:T(8,128)(2,1)S(1)}, u32[]{:S(2)}, u32[]{:S(2)}) collective-permute-start(bf16[512,512]{1,0:T(8,128)(2,1)} %shard_map.48.own_ref), channel_id=1, source_target_pairs={{0,1},{1,0},{2,3},{3,2},{4,5},{5,4},{6,7},{7,6},{8,9},{9,8},{10,11... | collective-permute-start | bytes 1572872 | tf_op jit(solution)/shard_map/ppermute | solution.py:357
  54.7 17.3 %collective-permute-start.10 = (bf16[16,16,512]{2,1,0:T(8,128)(2,1)S(1)}, bf16[16,16,512]{2,1,0:T(8,128)(2,1)S(1)}, u32[]{:S(2)}, u32[]{:S(2)}) collective-permute-start(bf16[16,16,512]{2,1,0:T(8,128)(2,1)S(1)} %all-to-all-done.a_hbm), channel_id=1, source_target_pairs={{0,384},{128,256},{256,128},{384,0},{1,385},{129,257},{257,129},{3... | collective-permute-start | bytes 786440 | tf_op jit(solution)/shard_map/ppermute | solution.py:361
  60.9 11.1 %collective-permute-start.9 = (bf16[16,16,512]{2,1,0:T(8,128)(2,1)S(1)}, bf16[16,16,512]{2,1,0:T(8,128)(2,1)S(1)}, u32[]{:S(2)}, u32[]{:S(2)}) collective-permute-start(bf16[16,16,512]{2,1,0:T(8,128)(2,1)S(1)} %all-to-all-done.a_hbm), channel_id=1, source_target_pairs={{0,256},{128,384},{256,0},{384,128},{1,257},{129,385},{257,1},{385... | collective-permute-start | bytes 786440 | tf_op jit(solution)/shard_map/ppermute | solution.py:361
  64.7 10.0 %collective-permute-start.8 = (bf16[16,16,512]{2,1,0:T(8,128)(2,1)S(1)}, bf16[16,16,512]{2,1,0:T(8,128)(2,1)S(1)}, u32[]{:S(2)}, u32[]{:S(2)}) collective-permute-start(bf16[16,16,512]{2,1,0:T(8,128)(2,1)S(1)} %all-to-all-done.a_hbm), channel_id=1, source_target_pairs={{0,128},{128,0},{256,384},{384,256},{1,129},{129,1},{257,385},{385... | collective-permute-start | bytes 786440 | tf_op jit(solution)/shard_map/ppermute | solution.py:361
  66.7 12.2 %collective-permute-start.6 = (bf16[256,512]{1,0:T(8,128)(2,1)S(1)}, bf16[256,512]{1,0:T(8,128)(2,1)S(1)}, u32[]{:S(2)}, u32[]{:S(2)}) collective-permute-start(bf16[256,512]{1,0:T(8,128)(2,1)S(1)} %slice.9), channel_id=1, source_target_pairs={{0,1},{1,0},{2,3},{3,2},{4,5},{5,4},{6,7},{7,6},{8,9},{9,8},{10,11... | collective-permute-start | bytes 786440 | tf_op jit(solution)/shard_map/ppermute | solution.py:369
  70.1 8.8 %collective-permute-start.5 = (bf16[256,512]{1,0:T(8,128)(2,1)S(1)}, bf16[256,512]{1,0:T(8,128)(2,1)S(1)}, u32[]{:S(2)}, u32[]{:S(2)}) collective-permute-start(bf16[256,512]{1,0:T(8,128)(2,1)S(1)} %slice.8), channel_id=1, source_target_pairs={{0,3},{1,2},{2,1},{3,0},{4,7},{5,6},{6,5},{7,4},{8,11},{9,10},{10,... | collective-permute-start | bytes 786440 | tf_op jit(solution)/shard_map/ppermute | solution.py:368
  74.8 6.3 %collective-permute-start.11 = (bf16[4,16,16,512]{3,2,1,0:T(8,128)(2,1)S(1)}, bf16[4,16,16,512]{3,2,1,0:T(8,128)(2,1)S(1)}, u32[]{:S(2)}, u32[]{:S(2)}) collective-permute-start(bf16[4,16,16,512]{3,2,1,0:T(8,128)(2,1)S(1)} %shard_map.52.mine_ref), channel_id=1, source_target_pairs={{0,4},{4,0},{8,12},{12,8},{16,20},{20,16},{24,28},{28,24},{32,36},... | collective-permute-start | bytes 3145736 | tf_op jit(solution)/shard_map/ppermute | solution.py:366
